TPU v7x, 32 devices: a whole 2x2x4 slice. The times are simulated.
32 devices in a mesh: groups: 2 (over y), rows: 4 (over z), cols: 2 (over x), sub: 2 (over core).
Axes of the slice: x: 2, y: 2, z: 4, core: 2. Of those that a mesh axis runs over, the one named last changes fastest.
Arguments:
- elevation: float32 [256, 16384], P(('groups', 'rows', 'sub'), 'cols'), parts along dimension 0, may hold values from -6 to 6
- fill_depth: float32 [256, 16384], P(('groups', 'rows', 'sub'), 'cols'), parts along dimension 0, may hold values from 0.5 to 4
- edge_rows: int32 [4, 16384], P('groups', 'cols'), parts along dimension 0, may hold values 0 or 1
- edge_sides: int32 [4, 128], P('groups', ('rows', 'sub')), parts along dimension 0, may hold values 0 or 1
- adjacency: int32 [16, 6], P('groups'), parts along dimension 0, may hold values from 0 to 7
Outputs:
- filled: float32 [256, 16384], P(('groups', 'rows', 'sub'), 'cols'), parts along dimension 0
There are 2 independent parts, one for each index of `groups`. A program takes and returns all parts, laid end to end along the dimension named above; each array names one. Nothing has to cross between parts.
Inputs may be any that keep to these rules, and one draw needn't show every extreme that they name: `adjacency`: tile numbers count tiles row by row.
All inputs are finite; a program needn't handle non-finite values. No bound on the sum of `edge_rows` or of `edge_sides` on one device may be relied on, other than what follows from the above.
Results may differ from a plain program's by a relative error of at most 0.00002.
Values sent between devices are 32-bit elements; how exact they have to be, the bound alone decides.
No kernel may reach another device: no remote copies, remote signals or barrier semaphores. Data moves between devices by JAX's collectives and lax.ppermute only.
A program may use at most 64 MiB of HBM per device.

v0:
```python
import jax
import jax.numpy as jnp
from jax import lax
from jax.experimental import pallas as pl
from jax.experimental.pallas import tpu as pltpu
from jax.sharding import PartitionSpec as P

PASSES = 8
FINAL = 4
ROUNDS = 4
SUBS = 8
LANES = 128
AHEAD = 5

unreached = 1000000000.0
rise_step = 0.01
hop_rise = 0.05
spill_lift = 3.0


def matching(count, first):
    pairs = []
    for low in range(first, count - 1, 2):
        pairs += [(low, low + 1), (low + 1, low)]
    return pairs


def cross(row_pairs, col_pairs, cols, subs):
    def device(place, col):
        return (place // subs * cols + col) * subs + place % subs

    return [
        (device(row, col), device(row_to, col_to))
        for row, row_to in row_pairs
        for col, col_to in col_pairs
    ]


def chain_place():
    subs = lax.axis_size("sub")
    return lax.axis_index("rows") * subs + lax.axis_index("sub"), lax.axis_size("rows") * subs


def position():
    sub = lax.broadcasted_iota(jnp.int32, (SUBS, LANES), 0)
    lane = lax.broadcasted_iota(jnp.int32, (SUBS, LANES), 1)
    return sub, lane


def aligned(start):
    return start if isinstance(start, int) else pl.multiple_of(start, SUBS)


def rows_at(first, count, size):
    return pl.ds(aligned(first * size), count * size)


def register(row, slot, size):
    return pl.ds(aligned(row * size + slot * SUBS), SUBS)


def side_marks(sides_ref):
    height = sides_ref.shape[1]
    square = (height, height)
    diagonal = lax.broadcasted_iota(jnp.int32, square, 0) == lax.broadcasted_iota(jnp.int32, square, 1)
    marks = sides_ref[...].astype(jnp.float32)
    return [
        jnp.sum(jnp.where(diagonal, marks[side : side + 1, :], 0.0), axis=1, keepdims=True)
        for side in range(2)
    ]


def start_all(copies):
    for copy in copies:
        copy.start()
    return copies


def wait_all(copies):
    for copy in copies:
        copy.wait()


def far_kernel(
    ground_hbm, depth_hbm, rows_hbm, sides_hbm,
    far_ref, far_even_ref, far_odd_ref, even_ref, odd_ref,
    ground_ref, depth_ref, edge_ref, marks_ref, sides_ref, sems, small_sems,
):
    height, width = ground_hbm.shape
    groups = height // SUBS
    tiles = width // (SUBS * LANES)
    last_tile = width // LANES - 1
    pieces = sems.shape[1]
    part = width // pieces
    place, places = chain_place()
    col, cols = lax.axis_index("cols"), lax.axis_size("cols")
    top = place % 2 == 0
    far_first = aligned(jnp.where(top, 0, height - SUBS))
    small = [pltpu.make_async_copy(sides_hbm, sides_ref, small_sems.at[0])]
    for side, tile in enumerate((0, last_tile)):
        columns = pl.ds(tile * LANES, LANES)
        for number, (source, target) in enumerate(
            (
                (ground_hbm.at[:, columns], edge_ref.at[side, 0]),
                (depth_hbm.at[:, columns], edge_ref.at[side, 1]),
                (rows_hbm.at[:, columns], marks_ref.at[side]),
            )
        ):
            small.append(pltpu.make_async_copy(source, target, small_sems.at[1 + side * 3 + number]))
    copies = []
    for piece in range(pieces):
        columns = pl.ds(piece * part, part)
        copies.append(
            [
                pltpu.make_async_copy(
                    source.at[pl.ds(far_first, SUBS), columns], target.at[:, columns], sems.at[kind, piece]
                )
                for kind, (source, target) in enumerate(((ground_hbm, ground_ref), (depth_hbm, depth_ref)))
            ]
        )
    start_all(copies[0])
    start_all(small)
    for pair in copies[1:]:
        start_all(pair)
    sub, lane = position()
    size = tiles * SUBS
    ground_base = jnp.where(top, 0, (SUBS - 1) * size)
    surface_base = jnp.where(top, (SUBS - 1) * size, 0)
    wait_all(copies[0])
    wait_all(small)
    marks = side_marks(sides_ref)
    shown = []
    for side in range(2):
        chosen = jnp.where(top, marks[side][:SUBS], marks[side][height - SUBS :])
        shown.append(
            (chosen > 0.5)
            & (lane == (0 if side == 0 else LANES - 1))
            & (col == (0 if side == 0 else cols - 1))
        )
    for tile in range(last_tile + 1):
        if tile and tile * LANES % part == 0:
            wait_all(copies[tile * LANES // part])
        columns = pl.ds(tile * LANES, LANES)
        ground = ground_ref[:, columns]
        surface = ground + depth_ref[:, columns]
        if tile == 0:
            surface = jnp.where(shown[0], ground, surface)
        if tile == last_tile:
            surface = jnp.where(shown[1], ground, surface)
        chunk, slot = tile // tiles, tile % tiles
        start = slot * SUBS + chunk
        far_ref[pl.ds(ground_base + start, SUBS, stride=size), :] = ground
        far_ref[pl.ds(surface_base + start, SUBS, stride=size), :] = surface
    rightward = col % 2 == 0
    strips = []
    for group in range(groups):
        rows = pl.ds(group * SUBS, SUBS)
        values = []
        for side in range(2):
            ground = edge_ref[side, 0, rows, :]
            surface = ground + edge_ref[side, 1, rows, :]
            outlet = (
                (marks[side][group * SUBS : (group + 1) * SUBS] > 0.5)
                & (lane == (0 if side == 0 else LANES - 1))
                & (col == (0 if side == 0 else cols - 1))
            )
            if group == 0:
                outlet = outlet | (marks_ref[side, 0:1] == 1) & (sub == 0) & (place == 0)
            if group == groups - 1:
                outlet = outlet | (marks_ref[side, 1:2] == 1) & (sub == SUBS - 1) & (place == places - 1)
            values.append((ground, jnp.where(outlet, ground, surface)))
        strips.append(values)
        for kind in range(2):
            rows = pl.ds(kind * height + group * SUBS, SUBS)
            even_ref[rows, :] = jnp.where(rightward, values[1][kind], values[0][kind])
            odd_ref[rows, :] = jnp.where(rightward, values[0][kind], values[1][kind])
    for kind in range(2):
        rows = pl.ds(kind * SUBS, SUBS)
        first, last = [jnp.where(top, strips[0][side][kind], strips[-1][side][kind]) for side in range(2)]
        far_even_ref[rows, :] = jnp.where(rightward, last, first)
        far_odd_ref[rows, :] = jnp.where(rightward, first, last)


def own_kernel(
    ground_hbm, depth_hbm, rows_hbm, sides_hbm, links_hbm, after_ref,
    ground_out, surface_out, near_ref, hops_ref,
    ground_ref, depth_ref, rows_ref, sides_ref, links_ref, sems, small_sems,
):
    height, width = ground_hbm.shape
    groups = height // SUBS
    tiles = width // (SUBS * LANES)
    last_tile = width // LANES - 1
    pieces = sems.shape[1] // groups
    part = width // pieces
    size = (tiles + 1) * SUBS
    copies = []
    for group in range(groups):
        for piece in range(pieces):
            where = (pl.ds(group * SUBS, SUBS), pl.ds(piece * part, part))
            number = group * pieces + piece
            copies.append(
                start_all(
                    [
                        pltpu.make_async_copy(ground_hbm.at[where], ground_ref.at[where], sems.at[0, number]),
                        pltpu.make_async_copy(depth_hbm.at[where], depth_ref.at[where], sems.at[1, number]),
                    ]
                )
            )
    small = start_all(
        [
            pltpu.make_async_copy(source, target, small_sems.at[number])
            for number, (source, target) in enumerate(
                ((rows_hbm, rows_ref), (sides_hbm, sides_ref), (links_hbm, links_ref))
            )
        ]
    )
    wait_all(small)
    hop_counts(links_ref, hops_ref, needed_tiles())
    place, places = chain_place()
    col, cols = lax.axis_index("cols"), lax.axis_size("cols")
    sub, lane = position()
    marks = side_marks(sides_ref)
    for group in range(groups):
        rows = pl.ds(group * SUBS, SUBS)
        for tile in range(last_tile + 1):
            if tile * LANES % part == 0:
                wait_all(copies[group * pieces + tile * LANES // part])
            columns = pl.ds(tile * LANES, LANES)
            ground = ground_ref[rows, columns]
            surface = ground + depth_ref[rows, columns]
            outlets = []
            if group == 0:
                outlets.append((rows_ref[0:1, columns] == 1) & (sub == 0) & (place == 0))
            if group == groups - 1:
                outlets.append(
                    (rows_ref[1:2, columns] == 1) & (sub == SUBS - 1) & (place == places - 1)
                )
            if tile == 0:
                outlets.append(
                    (marks[0][group * SUBS : (group + 1) * SUBS] > 0.5) & (lane == 0) & (col == 0)
                )
            if tile == last_tile:
                outlets.append(
                    (marks[1][group * SUBS : (group + 1) * SUBS] > 0.5)
                    & (lane == LANES - 1)
                    & (col == cols - 1)
                )
            for outlet in outlets:
                surface = jnp.where(outlet, ground, surface)
            chunk, slot = tile // tiles, tile % tiles
            start = (PASSES + group * SUBS) * size + slot * SUBS + chunk
            ground_out[pl.ds(start, SUBS, stride=size), :] = ground
            surface_out[pl.ds(start, SUBS, stride=size), :] = surface
    top = place % 2 == 0
    first = PASSES + jnp.where(top, height - SUBS, 0)
    packed = tiles * SUBS
    ground_base = jnp.where(top, SUBS - 1, 0)
    surface_base = jnp.where(top, 0, SUBS - 1)
    for source, base in ((ground_out, ground_base), (surface_out, surface_base)):
        for row in range(SUBS):
            for slot in range(tiles):
                near_ref[register(base + row, slot, packed), :] = source[register(first + row, slot, size), :]


def unpack_rows(rows_ref, first, is_top, present, strip_refs, strip_rows, ground_ref, surface_ref, tiles):
    packed = tiles * SUBS
    size = packed + SUBS
    bases = (jnp.where(is_top, SUBS - 1, 0), jnp.where(is_top, 0, SUBS - 1))
    for base, out_ref, strip_row in zip(bases, (ground_ref, surface_ref), strip_rows):

        def body(row, carry):
            values = [
                jnp.where(present, rows_ref[register(base + row, slot, packed), :], unreached)
                for slot in range(tiles)
            ]
            for slot in range(tiles):
                out_ref[register(first + row, slot, size), :] = values[slot]
            fill_seam(out_ref, first + row, values[0], values[-1], strip_refs, strip_row + row, present, tiles)
            return carry

        lax.fori_loop(0, PASSES, body, 0, unroll=4)


def fill_seam(out_ref, row, first_tile, last_tile, strip_refs, strip_row, present, tiles):
    col, cols = lax.axis_index("cols"), lax.axis_size("cols")
    sub, lane = position()
    rightward = col % 2 == 0
    even, odd = [ref[pl.ds(strip_row, 1), :] for ref in strip_refs]
    after = jnp.where(present & (col < cols - 1), jnp.where(rightward, even, odd), unreached)
    before = jnp.where(present & (col > 0), jnp.where(rightward, odd, even), unreached)
    after = jnp.where(sub == SUBS - 1, after, pltpu.roll(first_tile, SUBS - 1, 0))
    before = jnp.where(sub == 0, before, pltpu.roll(last_tile, 1, 0))
    out_ref[register(row, tiles, (tiles + 1) * SUBS), :] = jnp.where(lane < LANES // 2, after, before)


def relax_rows(source, target, ground, first, count, ring):
    size = ring * SUBS
    _, lane = position()
    at_first = lane == 0
    at_last = lane == LANES - 1
    order = [ring - 1] + list(range(ring - 1))
    made = {}

    def make(pair, slot):
        row = first + 2 * pair
        values = [source[register(row + step, slot, size), :] for step in range(-1, 3)]
        both = jnp.minimum(values[1], values[2])
        for one, column in enumerate((jnp.minimum(values[0], both), jnp.minimum(both, values[3]))):
            made[pair, one, slot] = (column, pltpu.roll(column, 1, 1), pltpu.roll(column, LANES - 1, 1))

    def finish(pair, slot):
        for one in range(2):
            row = first + 2 * pair + one
            before, here, after = [made[pair, one, (slot + step) % ring] for step in (-1, 0, 1)]
            from_left = jnp.where(at_first, before[1], here[1])
            from_right = jnp.where(at_last, after[2], here[2])
            lowest = jnp.minimum(jnp.minimum(from_left, from_right), here[0])
            where = register(row, slot, size)
            raised = jnp.minimum(source[where, :], lowest + rise_step)
            target[where, :] = jnp.maximum(ground[where, :], raised)

    makes = [(pair, slot) for pair in range(count // 2) for slot in order]
    finishes = [(pair, slot) for pair in range(count // 2) for slot in range(ring)]
    done = 0
    for number, item in enumerate(makes):
        make(*item)
        if number >= AHEAD:
            finish(*finishes[done])
            done += 1
    for item in finishes[done:]:
        finish(*item)


def hop_counts(links_ref, hops_ref, needed):
    tiles, degree = links_ref.shape
    links = links_ref[...]
    number = lax.broadcasted_iota(jnp.int32, (tiles, tiles), 1)
    linked = links[:, 0:1] == number
    for edge in range(1, degree):
        linked = linked | (links[:, edge : edge + 1] == number)
    linked = linked.astype(jnp.float32)
    tile = lax.broadcasted_iota(jnp.int32, (tiles, LANES), 0)
    lane = lax.broadcasted_iota(jnp.int32, (tiles, LANES), 1)
    reached = jnp.zeros((tiles, LANES), jnp.float32)
    for index, wanted in enumerate(needed):
        reached = jnp.where((lane == index) & (tile == wanted), 1.0, reached)
    hops = jnp.where(reached > 0.5, 0.0, float(ROUNDS + 1))
    for hop in range(1, ROUNDS + 1):
        reached = lax.dot_general(
            linked, reached, (((0,), (0,)), ((), ())), preferred_element_type=jnp.float32
        )
        reached = jnp.where(reached > 0.5, 1.0, 0.0)
        hops = jnp.minimum(hops, jnp.where(reached > 0.5, float(hop), float(ROUNDS + 1)))
    for index in range(len(needed)):
        hops_ref[pl.ds(index * tiles, tiles), :] = jnp.broadcast_to(
            hops[:, index : index + 1], (tiles, LANES)
        )


def needed_tiles():
    row, rows = lax.axis_index("rows"), lax.axis_size("rows")
    col, cols = lax.axis_index("cols"), lax.axis_size("cols")
    sub, subs = lax.axis_index("sub"), lax.axis_size("sub")
    above = jnp.maximum(jnp.where(sub == 0, row - 1, row), 0)
    below = jnp.minimum(jnp.where(sub == subs - 1, row + 1, row), rows - 1)
    left = jnp.maximum(col - 1, 0)
    right = jnp.minimum(col + 1, cols - 1)
    return [r * cols + c for r in (above, row, below) for c in (left, col, right)]


def inner_kernel(height, tiles, near_ref, *refs):
    own_strips, near_strips = refs[0:2], refs[2:4]
    ground_ref, surface_ref, other_ref = refs[6:9]
    ring = tiles + 1
    size = ring * SUBS
    place, places = chain_place()
    top = place % 2 == 0
    has_near = jnp.where(top, place < places - 1, place > 0)
    unpack_rows(
        near_ref,
        jnp.where(top, PASSES + height, 0),
        jnp.logical_not(top),
        has_near,
        near_strips,
        [kind * height + jnp.where(top, 0, height - SUBS) for kind in range(2)],
        ground_ref,
        surface_ref,
        tiles,
    )
    for kind, out_ref in enumerate((ground_ref, surface_ref)):

        def body(row, carry):
            first_tile = out_ref[register(PASSES + row, 0, size), :]
            last_tile = out_ref[register(PASSES + row, tiles - 1, size), :]
            fill_seam(
                out_ref, PASSES + row, first_tile, last_tile, own_strips, kind * height + row, place >= 0, tiles
            )
            return carry

        lax.fori_loop(0, height, body, 0, unroll=4)
    buffers = (surface_ref, other_ref)
    for step in range(1, PASSES + 1):
        first = step + jnp.where(top, PASSES, 0)
        count = height + PASSES - 2 * step
        relax_rows(buffers[(step + 1) % 2], buffers[step % 2], ground_ref, first, count, ring)


def outer_kernel(height, tiles, far_ref, even_ref, odd_ref, *refs):
    ground_ref, surface_ref, other_ref, level_ref, far_out, near_out = refs[3:9]
    ring = tiles + 1
    size = ring * SUBS
    place, places = chain_place()
    top = place % 2 == 0
    has_far = jnp.where(top, place > 0, place < places - 1)
    unpack_rows(
        far_ref,
        jnp.where(top, 0, PASSES + height),
        top,
        has_far,
        (even_ref, odd_ref),
        [0, SUBS],
        ground_ref,
        surface_ref,
        tiles,
    )
    buffers = (surface_ref, other_ref)
    for step in range(1, PASSES + 1):
        first = jnp.where(top, step, PASSES + height - step)
        relax_rows(buffers[(step + 1) % 2], buffers[step % 2], ground_ref, first, PASSES, ring)
    low, high = PASSES, PASSES + height - FINAL
    far_out[...] = surface_ref[rows_at(jnp.where(top, low, high), FINAL, size), :]
    near_out[...] = surface_ref[rows_at(jnp.where(top, high, low), FINAL, size), :]
    band, bands = lax.axis_index("sub"), lax.axis_size("sub")
    sub, lane = position()

    def at(row, slot):
        return surface_ref[register(PASSES + row, slot, size), :]

    first_cell = (sub == 0) & (lane == 0)
    last_cell = (sub == SUBS - 1) & (lane == LANES - 1)
    first_lows, last_lows, row_lows = [], [], []
    for row in range(height):
        first_lows.append(at(row, 0))
        last_lows.append(at(row, tiles - 1))
    for slot in range(tiles):
        row_lows.append(jnp.where(band == 0, at(0, slot), unreached))
        row_lows.append(jnp.where(band == bands - 1, at(height - 1, slot), unreached))
    lowest = jnp.minimum(
        least(row_lows),
        jnp.minimum(
            jnp.where(first_cell, least(first_lows), unreached),
            jnp.where(last_cell, least(last_lows), unreached),
        ),
    )
    lowest = jnp.min(jnp.min(lowest, axis=0, keepdims=True), axis=1, keepdims=True)
    tile_id = lax.axis_index("rows") * lax.axis_size("cols") + lax.axis_index("cols")
    number = lax.broadcasted_iota(jnp.int32, level_ref.shape, 0)
    level_ref[...] = jnp.where(number == tile_id, lowest, unreached)


def least(values):
    values = list(values)
    while len(values) > 1:
        values = [
            jnp.minimum(*values[number : number + 2]) if number + 1 < len(values) else values[number]
            for number in range(0, len(values), 2)
        ]
    return values[0]


def late_kernel(
    height, tiles, ground_ref, surface_ref, far_ref, near_ref, level_ref, hops_ref, out_hbm,
    one_ref, two_ref, out_ref, sems,
):
    ring = tiles + 1
    size = ring * SUBS
    sub, lane = position()
    place, _ = chain_place()
    top = place % 2 == 0
    level = level_ref[...]
    count = level.shape[0]
    raised = [level]
    for hop in range(ROUNDS):
        raised.append(raised[-1] + hop_rise)
    ceilings = []
    for index in range(9):
        hops = hops_ref[pl.ds(index * count, count), :]
        lowest = jnp.full((count, LANES), unreached, jnp.float32)
        for hop in range(ROUNDS + 1):
            lowest = jnp.where(hops == float(hop), raised[hop], lowest)
        lowest = jnp.min(lowest, axis=0, keepdims=True) + spill_lift
        ceilings.append(jnp.broadcast_to(lowest, (SUBS, LANES)))
    pairs = []
    for region in range(3):
        left, middle, right = ceilings[3 * region : 3 * region + 3]
        seam = jnp.where(
            lane < LANES // 2,
            jnp.where(sub == SUBS - 1, right, middle),
            jnp.where(sub == 0, left, middle),
        )
        pairs.append((middle, seam))
    low, high = PASSES - FINAL, PASSES + height
    far_pair = [jnp.where(top, above, below) for above, below in zip(pairs[0], pairs[2])]
    near_pair = [jnp.where(top, below, above) for above, below in zip(pairs[0], pairs[2])]
    spans = (
        (far_ref, 0, jnp.where(top, low, high), FINAL, far_pair),
        (near_ref, 0, jnp.where(top, high, low), FINAL, near_pair),
        (surface_ref, PASSES, PASSES, height, pairs[1]),
    )
    for source, source_first, first, rows, (middle, seam) in spans:

        def body(row, carry):
            for slot in range(ring):
                value = source[register(source_first + row, slot, size), :]
                value = jnp.minimum(value, seam if slot == tiles else middle)
                where = register(first + row, slot, size)
                one_ref[where, :] = jnp.maximum(ground_ref[where, :], value)
            return carry

        lax.fori_loop(0, rows, body, 0, unroll=4)
    buffers = (one_ref, two_ref)
    for step in range(1, FINAL):
        first = PASSES - FINAL + step
        relax_rows(
            buffers[(step + 1) % 2], buffers[step % 2], ground_ref, first, 2 * PASSES + height - 2 * first, ring
        )
    source, target = buffers[(FINAL + 1) % 2], buffers[FINAL % 2]
    copies = []
    for group in range(height // SUBS):
        first = PASSES + group * SUBS
        relax_rows(source, target, ground_ref, first, SUBS, ring)
        for tile in range(tiles * SUBS):
            chunk, slot = tile // tiles, tile % tiles
            out_ref[pl.ds(group * SUBS, SUBS), pl.ds(tile * LANES, LANES)] = target[
                pl.ds(first * size + slot * SUBS + chunk, SUBS, stride=size), :
            ]
        where = (pl.ds(group * SUBS, SUBS), slice(None))
        copies += start_all([pltpu.make_async_copy(out_ref.at[where], out_hbm.at[where], sems.at[group])])
    wait_all(copies)


def in_vmem(count):
    return [pl.BlockSpec(memory_space=pltpu.VMEM)] * count


def in_hbm(count):
    return [pl.BlockSpec(memory_space=pltpu.HBM)] * count


def exchange_stages(rows, cols, subs):
    bits = []
    for axis, count in enumerate((rows, cols, subs)):
        bit = 1
        while bit < count:
            bits.append((axis, bit))
            bit *= 2
    bits.reverse()
    stages = []
    for first in range(0, len(bits), 2):
        group = bits[first : first + 2]
        shifts = []
        for chosen in range(1, 2 ** len(group)):
            shift = [0, 0, 0]
            for number, (axis, bit) in enumerate(group):
                if chosen >> number & 1:
                    shift[axis] ^= bit
            shifts.append(shift)
        stages.append(shifts)
    return stages


def share_levels(level):
    rows, cols, subs = [lax.axis_size(axis) for axis in ("rows", "cols", "sub")]
    if any(count & (count - 1) for count in (rows, cols, subs)):
        return lax.pmin(level, ("rows", "cols", "sub"))
    for shifts in exchange_stages(rows, cols, subs):
        arrived = [level]
        for down, across, core in shifts:
            pairs = [
                (
                    (row * cols + col) * subs + sub,
                    ((row ^ down) * cols + (col ^ across)) * subs + (sub ^ core),
                )
                for row in range(rows)
                for col in range(cols)
                for sub in range(subs)
            ]
            arrived.append(lax.ppermute(level, ("rows", "cols", "sub"), pairs))
        level = least(arrived)
    return level


def per_device(elevation, fill_depth, edge_rows, edge_sides, adjacency):
    height, width = elevation.shape
    tiles = width // (SUBS * LANES)
    groups = height // SUBS
    f32 = jnp.float32
    packed = tiles * SUBS
    size = packed + SUBS
    tile_count = adjacency.shape[0]
    places = lax.axis_size(("rows", "sub"))
    cols, subs = lax.axis_size("cols"), lax.axis_size("sub")
    short = pl.CostEstimate(flops=1024, bytes_accessed=1024, transcendentals=0)
    limit = pltpu.CompilerParams(vmem_limit_bytes=24 << 20)
    arguments = [
        pltpu.with_memory_space_constraint(value, pltpu.HBM)
        for value in (elevation, fill_depth, edge_rows, edge_sides, adjacency)
    ]
    sent = pltpu.VMEM(((2 * PASSES - 1) * packed, LANES), f32)
    strip = pltpu.VMEM((2 * height, LANES), f32)
    far_strip = pltpu.VMEM((2 * SUBS, LANES), f32)
    far, far_even, far_odd, even, odd = pl.pallas_call(
        far_kernel,
        out_shape=[sent, far_strip, far_strip, strip, strip],
        in_specs=in_hbm(4),
        out_specs=in_vmem(5),
        scratch_shapes=[
            pltpu.VMEM((SUBS, width), f32),
            pltpu.VMEM((SUBS, width), f32),
            pltpu.VMEM((2, 2, height, LANES), f32),
            pltpu.VMEM((2, 2, LANES), jnp.int32),
            pltpu.VMEM(edge_sides.shape, jnp.int32),
            pltpu.SemaphoreType.DMA((2, 4)),
            pltpu.SemaphoreType.DMA((7,)),
        ],
        compiler_params=limit,
        cost_estimate=short,
        name="far_rows",
    )(*arguments[:4])

    near_pairs, far_pairs = matching(places, 0), matching(places, 1)
    stay = [(place, place) for place in range(places)]
    device_axes = ("rows", "cols", "sub")

    def swap_strips(pieces, row_pairs):
        arrived = []
        for first, piece in enumerate(pieces):
            pairs = cross(row_pairs, matching(cols, first), cols, subs)
            arrived.append(lax.ppermute(piece, device_axes, pairs) if pairs else piece)
        return arrived

    far_strips = swap_strips((far_even, far_odd), far_pairs)
    far_rows = lax.ppermute(far, ("rows", "sub"), far_pairs)

    work = pltpu.VMEM(((height + 2 * PASSES) * size, LANES), f32)
    ground, surface, near, hops = pl.pallas_call(
        own_kernel,
        out_shape=[work, work, sent, pltpu.VMEM((9 * tile_count, LANES), f32)],
        in_specs=in_hbm(5) + in_vmem(1),
        out_specs=in_vmem(4),
        scratch_shapes=[
            pltpu.VMEM((height, width), f32),
            pltpu.VMEM((height, width), f32),
            pltpu.VMEM(edge_rows.shape, jnp.int32),
            pltpu.VMEM(edge_sides.shape, jnp.int32),
            pltpu.VMEM(adjacency.shape, jnp.int32),
            pltpu.SemaphoreType.DMA((2, 4 * groups)),
            pltpu.SemaphoreType.DMA((3,)),
        ],
        compiler_params=limit,
        cost_estimate=short,
        name="own_rows",
    )(*arguments, far_even)

    near_rows = lax.ppermute(near, ("rows", "sub"), near_pairs)
    strips = swap_strips((even, odd), stay) + swap_strips((even, odd), near_pairs)

    def inner(near_ref, *refs):
        inner_kernel(height, tiles, near_ref, *refs)

    ground, surface, other = pl.pallas_call(
        inner,
        out_shape=[work, work, work],
        in_specs=in_vmem(7),
        out_specs=in_vmem(3),
        input_output_aliases={5: 0, 6: 1},
        compiler_params=limit,
        cost_estimate=short,
        name="inner_passes",
    )(near_rows, *strips, ground, surface)

    def outer(far_ref, *refs):
        outer_kernel(height, tiles, far_ref, *refs)

    again = pltpu.VMEM((FINAL * size, LANES), f32)
    ground, surface, other, level, far, near = pl.pallas_call(
        outer,
        out_shape=[work, work, work, pltpu.VMEM((tile_count, LANES), f32), again, again],
        in_specs=in_vmem(6),
        out_specs=in_vmem(6),
        input_output_aliases={3: 0, 4: 1, 5: 2},
        compiler_params=limit,
        cost_estimate=short,
        name="outer_passes",
    )(far_rows, *far_strips, ground, surface, other)

    far_rows = lax.ppermute(far, ("rows", "sub"), far_pairs)
    near_rows = lax.ppermute(near, ("rows", "sub"), near_pairs)
    level = share_levels(level)

    def late(*refs):
        late_kernel(height, tiles, *refs)

    return pl.pallas_call(
        late,
        out_shape=jax.ShapeDtypeStruct((height, width), f32),
        in_specs=in_vmem(6),
        out_specs=pl.BlockSpec(memory_space=pltpu.HBM),
        scratch_shapes=[
            pltpu.VMEM(((height + 2 * PASSES) * size, LANES), f32),
            pltpu.VMEM(((height + 2 * PASSES) * size, LANES), f32),
            pltpu.VMEM((height, width), f32),
            pltpu.SemaphoreType.DMA((groups,)),
        ],
        compiler_params=limit,
        cost_estimate=short,
        name="final_passes",
    )(ground, surface, far_rows, near_rows, level, hops)


def solution(mesh):
    placed = (
        P(("groups", "rows", "sub"), "cols"),
        P(("groups", "rows", "sub"), "cols"),
        P("groups", "cols"),
        P("groups", ("rows", "sub")),
        P("groups", None),
    )
    return jax.shard_map(
        per_device,
        mesh=mesh,
        in_specs=placed,
        out_specs=P(("groups", "rows", "sub"), "cols"),
        check_vma=False,
    )
```

profile of v0, /device:TPU:1, one launch (start us, length us, event | category | flops | bytes accessed | tf_op | source)
XLA Modules:
  0.0 35.8 jit_solution(6846154981303484117)
XLA Ops:
  0.0 1.4 %far_rows.1 = (f32[960,128]{1,0:T(8,128)S(1)}, f32[16,128]{1,0:T(8,128)S(1)}, f32[16,128]{1,0:T(8,128)S(1)}, f32[32,128]{1,0:T(8,128)S(1)}, f32[32,128]{1,0:T(8,128)S(1)}) custom-call(f32[16,8192]{1,0:T(8,128)} %ground_hbm.3, f32[16,8192]{1,0:T(8,128)} %depth_hbm.3, s32[2,8192]{1,0:T(2,128)} %rows_hbm.3, s32[2,16]{1,0:T(2,128)} %sides_hbm.3), custom_call_target="tpu_custom_call" | custom-call | flops 1024 | bytes 1024 | tf_op jit(solution)/shard_map/far_rows/pallas_call | solution.py:612
  1.4 2.4 %own_rows.1 = (f32[2304,128]{1,0:T(8,128)S(1)}, f32[2304,128]{1,0:T(8,128)S(1)}, f32[960,128]{1,0:T(8,128)S(1)}, f32[72,128]{1,0:T(8,128)S(1)}) custom-call(f32[16,8192]{1,0:T(8,128)} %ground_hbm.3, f32[16,8192]{1,0:T(8,128)} %depth_hbm.3, s32[2,8192]{1,0:T(2,128)} %rows_hbm.3, s32[2,16]{1,0:T(2,128)} %sides_hbm.3, s32[8,6]{1,0:T(8,128)} %links_hbm.1, ...), custom_call_target="tpu_custom_call" | custom-call | flops 1024 | bytes 1024 | tf_op jit(solution)/shard_map/own_rows/pallas_call | solution.py:646
  3.9 0.1 collective-permute-start.2
  4.0 4.6 %collective-permute-start = (f32[960,128]{1,0:T(8,128)S(1)}, f32[960,128]{1,0:T(8,128)S(1)}, u32[]{:S(2)}, u32[]{:S(2)}) collective-permute-start(f32[960,128]{1,0:T(8,128)S(1)} %get-tuple-element.22), channel_id=1, source_target_pairs={{1,4},{4,1},{5,8},{8,5},{9,12},{12,9},{3,6},{6,3},{7,10},{10,7},{1... | collective-permute-start | bytes 1474568 | tf_op jit(solution)/shard_map/ppermute | solution.py:643
  8.5 0.1 collective-permute-start.4
  8.6 1.3 %collective-permute-start.3 = (f32[32,128]{1,0:T(8,128)S(1)}, f32[32,128]{1,0:T(8,128)S(1)}, u32[]{:S(2)}, u32[]{:S(2)}) collective-permute-start(f32[32,128]{1,0:T(8,128)S(1)} %get-tuple-element.26), channel_id=1, source_target_pairs={{0,2},{2,0},{1,3},{3,1},{4,6},{6,4},{5,7},{7,5},{8,10},{10,8},{9,1... | collective-permute-start | bytes 49160 | tf_op jit(solution)/shard_map/ppermute | solution.py:639
  9.9 4.9 %collective-permute-start.1 = (f32[16,128]{1,0:T(8,128)S(1)}, f32[16,128]{1,0:T(8,128)S(1)}, u32[]{:S(2)}, u32[]{:S(2)}) collective-permute-start(f32[16,128]{1,0:T(8,128)S(1)} %get-tuple-element.23.after_ref), channel_id=1, source_target_pairs={{1,6},{3,4},{4,3},{6,1},{5,10},{7,8},{8,7},{10,5},{9,14},{11,12},{... | collective-permute-start | bytes 24584 | tf_op jit(solution)/shard_map/ppermute | solution.py:639
  14.8 0.0 collective-permute-done.4.refs_2_
  14.8 0.0 collective-permute-done.3.refs_0_
  14.8 0.0 collective-permute-done.2.near_ref
  14.8 2.8 %inner_passes.1 = (f32[2304,128]{1,0:T(8,128)S(1)}, f32[2304,128]{1,0:T(8,128)S(1)}, f32[2304,128]{1,0:T(8,128)S(1)}) custom-call(f32[960,128]{1,0:T(8,128)S(1)} %collective-permute-done.2.near_ref, f32[32,128]{1,0:T(8,128)S(1)} %collective-permute-done.3.refs_0_, ...), custom_call_target="tpu_custom_call", output_to_operand_aliasing={{0}: (5, {}), {1}: (6, {})} | custom-call | flops 1024 | bytes 1024 | tf_op jit(solution)/shard_map/inner_passes/pallas_call | solution.py:671
  17.6 0.0 collective-permute-done.1.refs_0_
  17.6 0.0 collective-permute-done.far_ref
  17.6 1.8 %outer_passes.1 = (f32[2304,128]{1,0:T(8,128)S(1)}, f32[2304,128]{1,0:T(8,128)S(1)}, f32[2304,128]{1,0:T(8,128)S(1)}, f32[8,128]{1,0:T(8,128)S(1)}, f32[288,128]{1,0:T(8,128)S(1)}, /*index=5*/f32[288,128]{1,0:T(8,128)S(1)}) custom-call(f32[960,128]{1,0:T(8,128)S(1)} %collective-permute-done.far_ref, ...), custom_call_target="tpu_custom_call", output_to_operand_aliasing={{0}: (3, {}), {1}: (4, {}), {2}: (5, {})} | custom-call | flops 1024 | bytes 1024 | tf_op jit(solution)/shard_map/outer_passes/pallas_call | solution.py:686
  19.4 0.0 collective-permute-start.9
  19.5 0.5 %collective-permute-start.8 = (f32[8,128]{1,0:T(8,128)S(1)}, f32[8,128]{1,0:T(8,128)S(1)}, u32[]{:S(2)}, u32[]{:S(2)}) collective-permute-start(f32[8,128]{1,0:T(8,128)S(1)} %get-tuple-element.37), channel_id=1, source_target_pairs={{0,2},{1,3},{2,0},{3,1},{4,6},{5,7},{6,4},{7,5},{8,10},{9,11},{10,... | collective-permute-start | bytes 12296 | tf_op jit(solution)/shard_map/ppermute | solution.py:588
  20.0 1.6 %collective-permute-start.7 = (f32[8,128]{1,0:T(8,128)S(1)}, f32[8,128]{1,0:T(8,128)S(1)}, u32[]{:S(2)}, u32[]{:S(2)}) collective-permute-start(f32[8,128]{1,0:T(8,128)S(1)} %get-tuple-element.37), channel_id=1, source_target_pairs={{0,1},{1,0},{2,3},{3,2},{4,5},{5,4},{6,7},{7,6},{8,9},{9,8},{10,11... | collective-permute-start | bytes 12296 | tf_op jit(solution)/shard_map/ppermute | solution.py:588
  21.6 0.9 %collective-permute-done.9 = f32[8,128]{1,0:T(8,128)S(1)} collective-permute-done((f32[8,128]{1,0:T(8,128)S(1)}, f32[8,128]{1,0:T(8,128)S(1)}, u32[]{:S(2)}, u32[]{:S(2)}) %collective-permute-start.9) | collective-permute-done | bytes 4128 | tf_op jit(solution)/shard_map/ppermute | solution.py:588
  22.5 0.0 collective-permute-done.8
  22.5 0.0 collective-permute-done.7
  22.5 1.9 %collective-permute-start.12 = (f32[8,128]{1,0:T(8,128)S(1)}, f32[8,128]{1,0:T(8,128)S(1)}, u32[]{:S(2)}, u32[]{:S(2)}) collective-permute-start(f32[8,128]{1,0:T(8,128)S(1)} %minimum_minimum_fusion.1), channel_id=1, source_target_pairs={{0,12},{1,13},{2,14},{3,15},{4,8},{5,9},{6,10},{7,11},{8,4},{9,5},... | collective-permute-start | bytes 12296 | tf_op jit(solution)/shard_map/ppermute | solution.py:588
  24.5 0.2 collective-permute-start.11
  24.7 1.5 %collective-permute-start.10 = (f32[8,128]{1,0:T(8,128)S(1)}, f32[8,128]{1,0:T(8,128)S(1)}, u32[]{:S(2)}, u32[]{:S(2)}) collective-permute-start(f32[8,128]{1,0:T(8,128)S(1)} %minimum_minimum_fusion.1), channel_id=1, source_target_pairs={{0,8},{1,9},{2,10},{3,11},{4,12},{5,13},{6,14},{7,15},{8,0},{9,1},... | collective-permute-start | bytes 12296 | tf_op jit(solution)/shard_map/ppermute | solution.py:588
  26.2 4.2 %collective-permute-start.5 = (f32[288,128]{1,0:T(8,128)S(1)}, f32[288,128]{1,0:T(8,128)S(1)}, u32[]{:S(2)}, u32[]{:S(2)}) collective-permute-start(f32[288,128]{1,0:T(8,128)S(1)} %get-tuple-element.35), channel_id=1, source_target_pairs={{1,4},{4,1},{5,8},{8,5},{9,12},{12,9},{3,6},{6,3},{7,10},{10,7},{1... | collective-permute-start | bytes 442376 | tf_op jit(solution)/shard_map/ppermute | solution.py:697
  30.4 0.1 collective-permute-start.6
  30.5 0.0 collective-permute-done.12
  30.5 0.0 collective-permute-done.11
  30.5 0.0 collective-permute-done.10
  30.5 2.7 %collective-permute-done.5.refs_2_ = f32[288,128]{1,0:T(8,128)S(1)} collective-permute-done((f32[288,128]{1,0:T(8,128)S(1)}, f32[288,128]{1,0:T(8,128)S(1)}, u32[]{:S(2)}, u32[]{:S(2)}) %collective-permute-start.5) | collective-permute-done | bytes 147488 | tf_op jit(solution)/shard_map/ppermute | solution.py:697
  33.2 0.0 collective-permute-done.6.refs_3_
  33.2 2.6 %final_passes.1 = f32[16,8192]{1,0:T(8,128)} custom-call(f32[2304,128]{1,0:T(8,128)S(1)} %get-tuple-element.33.refs_0_, f32[2304,128]{1,0:T(8,128)S(1)} %get-tuple-element.34.refs_1_, f32[288,128]{1,0:T(8,128)S(1)} %collective-permute-done.5.refs_2_, f32[288,128]{1,0:T(8,128)S(1)} %collective-permute-done.6.refs_3_, ...), custom_call_target="tpu_custom_call" | custom-call | flops 1024 | bytes 1024 | tf_op jit(solution)/shard_map/final_passes/pallas_call | solution.py:704
  (2 shorter events, 0.0 us)
Async XLA Ops:
  3.9 10.9 %collective-permute-start.2 = (f32[960,128]{1,0:T(8,128)S(1)}, f32[960,128]{1,0:T(8,128)S(1)}, u32[]{:S(2)}, u32[]{:S(2)}) collective-permute-start(f32[960,128]{1,0:T(8,128)S(1)} %get-tuple-element.25), channel_id=1, source_target_pairs={{0,1},{1,0},{4,5},{5,4},{8,9},{9,8},{12,13},{13,12},{2,3},{3,2},{6... | collective-permute-start | bytes 1474568 | tf_op jit(solution)/shard_map/ppermute | solution.py:665
  4.0 13.7 %collective-permute-start = (f32[960,128]{1,0:T(8,128)S(1)}, f32[960,128]{1,0:T(8,128)S(1)}, u32[]{:S(2)}, u32[]{:S(2)}) collective-permute-start(f32[960,128]{1,0:T(8,128)S(1)} %get-tuple-element.22), channel_id=1, source_target_pairs={{1,4},{4,1},{5,8},{8,5},{9,12},{12,9},{3,6},{6,3},{7,10},{10,7},{1... | collective-permute-start | bytes 1474568 | tf_op jit(solution)/shard_map/ppermute | solution.py:643
  8.5 6.2 %collective-permute-start.4 = (f32[32,128]{1,0:T(8,128)S(1)}, f32[32,128]{1,0:T(8,128)S(1)}, u32[]{:S(2)}, u32[]{:S(2)}) collective-permute-start(f32[32,128]{1,0:T(8,128)S(1)} %get-tuple-element.26), channel_id=1, source_target_pairs={{0,3},{2,1},{1,2},{3,0},{4,7},{6,5},{5,6},{7,4},{8,11},{10,9},{9,1... | collective-permute-start | bytes 49160 | tf_op jit(solution)/shard_map/ppermute | solution.py:639
  8.6 6.2 %collective-permute-start.3 = (f32[32,128]{1,0:T(8,128)S(1)}, f32[32,128]{1,0:T(8,128)S(1)}, u32[]{:S(2)}, u32[]{:S(2)}) collective-permute-start(f32[32,128]{1,0:T(8,128)S(1)} %get-tuple-element.26), channel_id=1, source_target_pairs={{0,2},{2,0},{1,3},{3,1},{4,6},{6,4},{5,7},{7,5},{8,10},{10,8},{9,1... | collective-permute-start | bytes 49160 | tf_op jit(solution)/shard_map/ppermute | solution.py:639
  9.9 7.7 %collective-permute-start.1 = (f32[16,128]{1,0:T(8,128)S(1)}, f32[16,128]{1,0:T(8,128)S(1)}, u32[]{:S(2)}, u32[]{:S(2)}) collective-permute-start(f32[16,128]{1,0:T(8,128)S(1)} %get-tuple-element.23.after_ref), channel_id=1, source_target_pairs={{1,6},{3,4},{4,3},{6,1},{5,10},{7,8},{8,7},{10,5},{9,14},{11,12},{... | collective-permute-start | bytes 24584 | tf_op jit(solution)/shard_map/ppermute | solution.py:639
  19.4 3.1 %collective-permute-start.9 = (f32[8,128]{1,0:T(8,128)S(1)}, f32[8,128]{1,0:T(8,128)S(1)}, u32[]{:S(2)}, u32[]{:S(2)}) collective-permute-start(f32[8,128]{1,0:T(8,128)S(1)} %get-tuple-element.37), channel_id=1, source_target_pairs={{0,3},{1,2},{2,1},{3,0},{4,7},{5,6},{6,5},{7,4},{8,11},{9,10},{10,... | collective-permute-start | bytes 12296 | tf_op jit(solution)/shard_map/ppermute | solution.py:588
  19.5 3.0 %collective-permute-start.8 = (f32[8,128]{1,0:T(8,128)S(1)}, f32[8,128]{1,0:T(8,128)S(1)}, u32[]{:S(2)}, u32[]{:S(2)}) collective-permute-start(f32[8,128]{1,0:T(8,128)S(1)} %get-tuple-element.37), channel_id=1, source_target_pairs={{0,2},{1,3},{2,0},{3,1},{4,6},{5,7},{6,4},{7,5},{8,10},{9,11},{10,... | collective-permute-start | bytes 12296 | tf_op jit(solution)/shard_map/ppermute | solution.py:588
  20.0 2.5 %collective-permute-start.7 = (f32[8,128]{1,0:T(8,128)S(1)}, f32[8,128]{1,0:T(8,128)S(1)}, u32[]{:S(2)}, u32[]{:S(2)}) collective-permute-start(f32[8,128]{1,0:T(8,128)S(1)} %get-tuple-element.37), channel_id=1, source_target_pairs={{0,1},{1,0},{2,3},{3,2},{4,5},{5,4},{6,7},{7,6},{8,9},{9,8},{10,11... | collective-permute-start | bytes 12296 | tf_op jit(solution)/shard_map/ppermute | solution.py:588
  22.5 7.9 %collective-permute-start.12 = (f32[8,128]{1,0:T(8,128)S(1)}, f32[8,128]{1,0:T(8,128)S(1)}, u32[]{:S(2)}, u32[]{:S(2)}) collective-permute-start(f32[8,128]{1,0:T(8,128)S(1)} %minimum_minimum_fusion.1), channel_id=1, source_target_pairs={{0,12},{1,13},{2,14},{3,15},{4,8},{5,9},{6,10},{7,11},{8,4},{9,5},... | collective-permute-start | bytes 12296 | tf_op jit(solution)/shard_map/ppermute | solution.py:588
  24.5 6.0 %collective-permute-start.11 = (f32[8,128]{1,0:T(8,128)S(1)}, f32[8,128]{1,0:T(8,128)S(1)}, u32[]{:S(2)}, u32[]{:S(2)}) collective-permute-start(f32[8,128]{1,0:T(8,128)S(1)} %minimum_minimum_fusion.1), channel_id=1, source_target_pairs={{0,4},{1,5},{2,6},{3,7},{4,0},{5,1},{6,2},{7,3},{8,12},{9,13},{10,... | collective-permute-start | bytes 12296 | tf_op jit(solution)/shard_map/ppermute | solution.py:588
  24.7 5.8 %collective-permute-start.10 = (f32[8,128]{1,0:T(8,128)S(1)}, f32[8,128]{1,0:T(8,128)S(1)}, u32[]{:S(2)}, u32[]{:S(2)}) collective-permute-start(f32[8,128]{1,0:T(8,128)S(1)} %minimum_minimum_fusion.1), channel_id=1, source_target_pairs={{0,8},{1,9},{2,10},{3,11},{4,12},{5,13},{6,14},{7,15},{8,0},{9,1},... | collective-permute-start | bytes 12296 | tf_op jit(solution)/shard_map/ppermute | solution.py:588
  26.2 7.1 %collective-permute-start.5 = (f32[288,128]{1,0:T(8,128)S(1)}, f32[288,128]{1,0:T(8,128)S(1)}, u32[]{:S(2)}, u32[]{:S(2)}) collective-permute-start(f32[288,128]{1,0:T(8,128)S(1)} %get-tuple-element.35), channel_id=1, source_target_pairs={{1,4},{4,1},{5,8},{8,5},{9,12},{12,9},{3,6},{6,3},{7,10},{10,7},{1... | collective-permute-start | bytes 442376 | tf_op jit(solution)/shard_map/ppermute | solution.py:697
  30.4 2.8 %collective-permute-start.6 = (f32[288,128]{1,0:T(8,128)S(1)}, f32[288,128]{1,0:T(8,128)S(1)}, u32[]{:S(2)}, u32[]{:S(2)}) collective-permute-start(f32[288,128]{1,0:T(8,128)S(1)} %get-tuple-element.36), channel_id=1, source_target_pairs={{0,1},{1,0},{4,5},{5,4},{8,9},{9,8},{12,13},{13,12},{2,3},{3,2},{6... | collective-permute-start | bytes 442376 | tf_op jit(solution)/shard_map/ppermute | solution.py:698
where the time goes:
time: 36 us; the launch traced here: 35.8 us
  starting transfers between devices  21 us (58%)
  Pallas kernels  11 us (31%)
  waiting for transfers between devices  3.61 us (10%)
    ppermute x2, starting transfers between devices, per_device(): far_rows = lax.ppermute(far, ('rows', 'sub'), far_pairs)  8.79 us
    ppermute x3, starting transfers between devices, swap_strips(): arrived.append(lax.ppermute(piece, device_axes, pairs) if pairs else piece)  6.2 us
    ppermute x6, starting transfers between devices, share_levels(): arrived.append(lax.ppermute(level, ('rows', 'cols', 'sub'), pairs))  5.79 us
    pallas_call x1, Pallas kernels, per_device(): pl.pallas_call(inner, out_shape=[work, work, work], in_specs=in_vmem(7),...  2.82 us
    ppermute x2, waiting for transfers between devices, per_device(): far_rows = lax.ppermute(far, ('rows', 'sub'), far_pairs)  2.69 us
    pallas_call x1, Pallas kernels, per_device(): pl.pallas_call(late, out_shape=jax.ShapeDtypeStruct((height, width), f32)...  2.56 us
    pallas_call x1, Pallas kernels, per_device(): pl.pallas_call(own_kernel, out_shape=[work, work, sent, pltpu.VMEM((9 * t...  2.41 us
    pallas_call x1, Pallas kernels, per_device(): pl.pallas_call(outer, out_shape=[work, work, work, pltpu.VMEM((tile_count...  1.81 us
  transfers between devices with their start and end apart: 13, of which 2 were waited for; matrix products, arithmetic and copies ran while one was open for 0% of the time, Pallas kernels for 8%

commit v1 on v0

--- a/solution.py
+++ b/solution.py
@@ -81,21 +81,21 @@
         copy.wait()
 
 
-def far_kernel(
+def edge_kernel(
     ground_hbm, depth_hbm, rows_hbm, sides_hbm,
-    far_ref, far_even_ref, far_odd_ref, even_ref, odd_ref,
+    far_ref, near_ref, far_even_ref, far_odd_ref, even_ref, odd_ref,
     ground_ref, depth_ref, edge_ref, marks_ref, sides_ref, sems, small_sems,
 ):
     height, width = ground_hbm.shape
     groups = height // SUBS
     tiles = width // (SUBS * LANES)
     last_tile = width // LANES - 1
-    pieces = sems.shape[1]
+    pieces = sems.shape[2]
     part = width // pieces
     place, places = chain_place()
     col, cols = lax.axis_index("cols"), lax.axis_size("cols")
     top = place % 2 == 0
-    far_first = aligned(jnp.where(top, 0, height - SUBS))
+    firsts = [aligned(jnp.where(is_top, 0, height - SUBS)) for is_top in (top, jnp.logical_not(top))]
     small = [pltpu.make_async_copy(sides_hbm, sides_ref, small_sems.at[0])]
     for side, tile in enumerate((0, last_tile)):
         columns = pl.ds(tile * LANES, LANES)
@@ -107,50 +107,46 @@
             )
         ):
             small.append(pltpu.make_async_copy(source, target, small_sems.at[1 + side * 3 + number]))
-    copies = []
-    for piece in range(pieces):
-        columns = pl.ds(piece * part, part)
-        copies.append(
+    copies = [
+        [
             [
                 pltpu.make_async_copy(
-                    source.at[pl.ds(far_first, SUBS), columns], target.at[:, columns], sems.at[kind, piece]
+                    source.at[pl.ds(first, SUBS), pl.ds(piece * part, part)],
+                    target.at[where, :, pl.ds(piece * part, part)],
+                    sems.at[where, kind, piece],
                 )
                 for kind, (source, target) in enumerate(((ground_hbm, ground_ref), (depth_hbm, depth_ref)))
             ]
-        )
-    start_all(copies[0])
+            for piece in range(pieces)
+        ]
+        for where, first in enumerate(firsts)
+    ]
+    start_all(copies[0][0])
     start_all(small)
-    for pair in copies[1:]:
+    for pair in copies[0][1:] + copies[1]:
         start_all(pair)
     sub, lane = position()
     size = tiles * SUBS
-    ground_base = jnp.where(top, 0, (SUBS - 1) * size)
-    surface_base = jnp.where(top, (SUBS - 1) * size, 0)
-    wait_all(copies[0])
     wait_all(small)
     marks = side_marks(sides_ref)
-    shown = []
-    for side in range(2):
-        chosen = jnp.where(top, marks[side][:SUBS], marks[side][height - SUBS :])
-        shown.append(
-            (chosen > 0.5)
-            & (lane == (0 if side == 0 else LANES - 1))
-            & (col == (0 if side == 0 else cols - 1))
-        )
-    for tile in range(last_tile + 1):
-        if tile and tile * LANES % part == 0:
-            wait_all(copies[tile * LANES // part])
-        columns = pl.ds(tile * LANES, LANES)
-        ground = ground_ref[:, columns]
-        surface = ground + depth_ref[:, columns]
-        if tile == 0:
-            surface = jnp.where(shown[0], ground, surface)
-        if tile == last_tile:
-            surface = jnp.where(shown[1], ground, surface)
-        chunk, slot = tile // tiles, tile % tiles
-        start = slot * SUBS + chunk
-        far_ref[pl.ds(ground_base + start, SUBS, stride=size), :] = ground
-        far_ref[pl.ds(surface_base + start, SUBS, stride=size), :] = surface
+    at_edges = [(lane == 0) & (col == 0), (lane == LANES - 1) & (col == cols - 1)]
+    for where, (out_ref, is_top) in enumerate(((far_ref, top), (near_ref, jnp.logical_not(top)))):
+        ground_base = jnp.where(is_top, 0, (SUBS - 1) * size)
+        surface_base = jnp.where(is_top, (SUBS - 1) * size, 0)
+        for tile in range(last_tile + 1):
+            if tile * LANES % part == 0:
+                wait_all(copies[where][tile * LANES // part])
+            columns = pl.ds(tile * LANES, LANES)
+            ground = ground_ref[where, :, columns]
+            surface = ground + depth_ref[where, :, columns]
+            if tile in (0, last_tile):
+                side = 0 if tile == 0 else 1
+                chosen = jnp.where(is_top, marks[side][:SUBS], marks[side][height - SUBS :])
+                surface = jnp.where((chosen > 0.5) & at_edges[side], ground, surface)
+            chunk, slot = tile // tiles, tile % tiles
+            start = slot * SUBS + chunk
+            out_ref[pl.ds(ground_base + start, SUBS, stride=size), :] = ground
+            out_ref[pl.ds(surface_base + start, SUBS, stride=size), :] = surface
     rightward = col % 2 == 0
     strips = []
     for group in range(groups):
@@ -159,11 +155,7 @@
         for side in range(2):
             ground = edge_ref[side, 0, rows, :]
             surface = ground + edge_ref[side, 1, rows, :]
-            outlet = (
-                (marks[side][group * SUBS : (group + 1) * SUBS] > 0.5)
-                & (lane == (0 if side == 0 else LANES - 1))
-                & (col == (0 if side == 0 else cols - 1))
-            )
+            outlet = (marks[side][group * SUBS : (group + 1) * SUBS] > 0.5) & at_edges[side]
             if group == 0:
                 outlet = outlet | (marks_ref[side, 0:1] == 1) & (sub == 0) & (place == 0)
             if group == groups - 1:
@@ -181,18 +173,11 @@
         far_odd_ref[rows, :] = jnp.where(rightward, first, last)
 
 
-def own_kernel(
-    ground_hbm, depth_hbm, rows_hbm, sides_hbm, links_hbm, after_ref,
-    ground_out, surface_out, near_ref, hops_ref,
-    ground_ref, depth_ref, rows_ref, sides_ref, links_ref, sems, small_sems,
-):
+def start_own(ground_hbm, depth_hbm, ground_ref, depth_ref, sems):
     height, width = ground_hbm.shape
     groups = height // SUBS
-    tiles = width // (SUBS * LANES)
-    last_tile = width // LANES - 1
     pieces = sems.shape[1] // groups
     part = width // pieces
-    size = (tiles + 1) * SUBS
     copies = []
     for group in range(groups):
         for piece in range(pieces):
@@ -206,16 +191,17 @@
                     ]
                 )
             )
-    small = start_all(
-        [
-            pltpu.make_async_copy(source, target, small_sems.at[number])
-            for number, (source, target) in enumerate(
-                ((rows_hbm, rows_ref), (sides_hbm, sides_ref), (links_hbm, links_ref))
-            )
-        ]
-    )
-    wait_all(small)
-    hop_counts(links_ref, hops_ref, needed_tiles())
+    return copies
+
+
+def fold_own(copies, ground_ref, depth_ref, rows_ref, sides_ref, ground_out, surface_out):
+    height, width = ground_ref.shape
+    groups = height // SUBS
+    tiles = width // (SUBS * LANES)
+    last_tile = width // LANES - 1
+    pieces = len(copies) // groups
+    part = width // pieces
+    size = (tiles + 1) * SUBS
     place, places = chain_place()
     col, cols = lax.axis_index("cols"), lax.axis_size("cols")
     sub, lane = position()
@@ -251,15 +237,6 @@
             start = (PASSES + group * SUBS) * size + slot * SUBS + chunk
             ground_out[pl.ds(start, SUBS, stride=size), :] = ground
             surface_out[pl.ds(start, SUBS, stride=size), :] = surface
-    top = place % 2 == 0
-    first = PASSES + jnp.where(top, height - SUBS, 0)
-    packed = tiles * SUBS
-    ground_base = jnp.where(top, SUBS - 1, 0)
-    surface_base = jnp.where(top, 0, SUBS - 1)
-    for source, base in ((ground_out, ground_base), (surface_out, surface_base)):
-        for row in range(SUBS):
-            for slot in range(tiles):
-                near_ref[register(base + row, slot, packed), :] = source[register(first + row, slot, size), :]
 
 
 def unpack_rows(rows_ref, first, is_top, present, strip_refs, strip_rows, ground_ref, surface_ref, tiles):
@@ -368,9 +345,24 @@
     return [r * cols + c for r in (above, row, below) for c in (left, col, right)]
 
 
-def inner_kernel(height, tiles, near_ref, *refs):
-    own_strips, near_strips = refs[0:2], refs[2:4]
-    ground_ref, surface_ref, other_ref = refs[6:9]
+def inner_kernel(
+    ground_hbm, depth_hbm, rows_hbm, sides_hbm, links_hbm,
+    near_ref, own_even_ref, own_odd_ref, near_even_ref, near_odd_ref,
+    ground_ref, surface_ref, other_ref, hops_ref,
+    raw_ground_ref, raw_depth_ref, rows_ref, sides_ref, links_ref, sems, small_sems,
+):
+    height, width = ground_hbm.shape
+    tiles = width // (SUBS * LANES)
+    small = start_all(
+        [
+            pltpu.make_async_copy(source, target, small_sems.at[number])
+            for number, (source, target) in enumerate(
+                ((rows_hbm, rows_ref), (sides_hbm, sides_ref), (links_hbm, links_ref))
+            )
+        ]
+    )
+    copies = start_own(ground_hbm, depth_hbm, raw_ground_ref, raw_depth_ref, sems)
+    own_strips, near_strips = (own_even_ref, own_odd_ref), (near_even_ref, near_odd_ref)
     ring = tiles + 1
     size = ring * SUBS
     place, places = chain_place()
@@ -387,6 +379,9 @@
         surface_ref,
         tiles,
     )
+    wait_all(small)
+    hop_counts(links_ref, hops_ref, needed_tiles())
+    fold_own(copies, raw_ground_ref, raw_depth_ref, rows_ref, sides_ref, ground_ref, surface_ref)
     for kind, out_ref in enumerate((ground_ref, surface_ref)):
 
         def body(row, carry):
@@ -453,9 +448,7 @@
         ),
     )
     lowest = jnp.min(jnp.min(lowest, axis=0, keepdims=True), axis=1, keepdims=True)
-    tile_id = lax.axis_index("rows") * lax.axis_size("cols") + lax.axis_index("cols")
-    number = lax.broadcasted_iota(jnp.int32, level_ref.shape, 0)
-    level_ref[...] = jnp.where(number == tile_id, lowest, unreached)
+    level_ref[...] = jnp.broadcast_to(lowest, level_ref.shape)
 
 
 def least(values):
@@ -469,7 +462,7 @@
 
 
 def late_kernel(
-    height, tiles, ground_ref, surface_ref, far_ref, near_ref, level_ref, hops_ref, out_hbm,
+    height, tiles, ground_ref, surface_ref, far_ref, near_ref, floors_ref, hops_ref, out_hbm,
     one_ref, two_ref, out_ref, sems,
 ):
     ring = tiles + 1
@@ -477,8 +470,9 @@
     sub, lane = position()
     place, _ = chain_place()
     top = place % 2 == 0
-    level = level_ref[...]
-    count = level.shape[0]
+    bands = lax.axis_size("sub")
+    count = floors_ref.shape[0] // (bands * SUBS)
+    level = least(floors_ref[pl.ds(band * SUBS, count, stride=bands * SUBS), :] for band in range(bands))
     raised = [level]
     for hop in range(ROUNDS):
         raised.append(raised[-1] + hop_rise)
@@ -547,49 +541,6 @@
     return [pl.BlockSpec(memory_space=pltpu.HBM)] * count
 
 
-def exchange_stages(rows, cols, subs):
-    bits = []
-    for axis, count in enumerate((rows, cols, subs)):
-        bit = 1
-        while bit < count:
-            bits.append((axis, bit))
-            bit *= 2
-    bits.reverse()
-    stages = []
-    for first in range(0, len(bits), 2):
-        group = bits[first : first + 2]
-        shifts = []
-        for chosen in range(1, 2 ** len(group)):
-            shift = [0, 0, 0]
-            for number, (axis, bit) in enumerate(group):
-                if chosen >> number & 1:
-                    shift[axis] ^= bit
-            shifts.append(shift)
-        stages.append(shifts)
-    return stages
-
-
-def share_levels(level):
-    rows, cols, subs = [lax.axis_size(axis) for axis in ("rows", "cols", "sub")]
-    if any(count & (count - 1) for count in (rows, cols, subs)):
-        return lax.pmin(level, ("rows", "cols", "sub"))
-    for shifts in exchange_stages(rows, cols, subs):
-        arrived = [level]
-        for down, across, core in shifts:
-            pairs = [
-                (
-                    (row * cols + col) * subs + sub,
-                    ((row ^ down) * cols + (col ^ across)) * subs + (sub ^ core),
-                )
-                for row in range(rows)
-                for col in range(cols)
-                for sub in range(subs)
-            ]
-            arrived.append(lax.ppermute(level, ("rows", "cols", "sub"), pairs))
-        level = least(arrived)
-    return level
-
-
 def per_device(elevation, fill_depth, edge_rows, edge_sides, adjacency):
     height, width = elevation.shape
     tiles = width // (SUBS * LANES)
@@ -609,23 +560,23 @@
     sent = pltpu.VMEM(((2 * PASSES - 1) * packed, LANES), f32)
     strip = pltpu.VMEM((2 * height, LANES), f32)
     far_strip = pltpu.VMEM((2 * SUBS, LANES), f32)
-    far, far_even, far_odd, even, odd = pl.pallas_call(
-        far_kernel,
-        out_shape=[sent, far_strip, far_strip, strip, strip],
+    far, near, far_even, far_odd, even, odd = pl.pallas_call(
+        edge_kernel,
+        out_shape=[sent, sent, far_strip, far_strip, strip, strip],
         in_specs=in_hbm(4),
-        out_specs=in_vmem(5),
+        out_specs=in_vmem(6),
         scratch_shapes=[
-            pltpu.VMEM((SUBS, width), f32),
-            pltpu.VMEM((SUBS, width), f32),
+            pltpu.VMEM((2, SUBS, width), f32),
+            pltpu.VMEM((2, SUBS, width), f32),
             pltpu.VMEM((2, 2, height, LANES), f32),
             pltpu.VMEM((2, 2, LANES), jnp.int32),
             pltpu.VMEM(edge_sides.shape, jnp.int32),
-            pltpu.SemaphoreType.DMA((2, 4)),
+            pltpu.SemaphoreType.DMA((2, 2, 4)),
             pltpu.SemaphoreType.DMA((7,)),
         ],
         compiler_params=limit,
         cost_estimate=short,
-        name="far_rows",
+        name="edge_rows",
     )(*arguments[:4])
 
     near_pairs, far_pairs = matching(places, 0), matching(places, 1)
@@ -641,12 +592,14 @@
 
     far_strips = swap_strips((far_even, far_odd), far_pairs)
     far_rows = lax.ppermute(far, ("rows", "sub"), far_pairs)
+    near_rows = lax.ppermute(near, ("rows", "sub"), near_pairs)
+    strips = swap_strips((even, odd), stay) + swap_strips((even, odd), near_pairs)
 
     work = pltpu.VMEM(((height + 2 * PASSES) * size, LANES), f32)
-    ground, surface, near, hops = pl.pallas_call(
-        own_kernel,
-        out_shape=[work, work, sent, pltpu.VMEM((9 * tile_count, LANES), f32)],
-        in_specs=in_hbm(5) + in_vmem(1),
+    ground, surface, other, hops = pl.pallas_call(
+        inner_kernel,
+        out_shape=[work, work, work, pltpu.VMEM((9 * tile_count, LANES), f32)],
+        in_specs=in_hbm(5) + in_vmem(5),
         out_specs=in_vmem(4),
         scratch_shapes=[
             pltpu.VMEM((height, width), f32),
@@ -659,25 +612,8 @@
         ],
         compiler_params=limit,
         cost_estimate=short,
-        name="own_rows",
-    )(*arguments, far_even)
-
-    near_rows = lax.ppermute(near, ("rows", "sub"), near_pairs)
-    strips = swap_strips((even, odd), stay) + swap_strips((even, odd), near_pairs)
-
-    def inner(near_ref, *refs):
-        inner_kernel(height, tiles, near_ref, *refs)
-
-    ground, surface, other = pl.pallas_call(
-        inner,
-        out_shape=[work, work, work],
-        in_specs=in_vmem(7),
-        out_specs=in_vmem(3),
-        input_output_aliases={5: 0, 6: 1},
-        compiler_params=limit,
-        cost_estimate=short,
         name="inner_passes",
-    )(near_rows, *strips, ground, surface)
+    )(*arguments, near_rows, *strips)
 
     def outer(far_ref, *refs):
         outer_kernel(height, tiles, far_ref, *refs)
@@ -685,7 +621,7 @@
     again = pltpu.VMEM((FINAL * size, LANES), f32)
     ground, surface, other, level, far, near = pl.pallas_call(
         outer,
-        out_shape=[work, work, work, pltpu.VMEM((tile_count, LANES), f32), again, again],
+        out_shape=[work, work, work, pltpu.VMEM((SUBS, LANES), f32), again, again],
         in_specs=in_vmem(6),
         out_specs=in_vmem(6),
         input_output_aliases={3: 0, 4: 1, 5: 2},
@@ -694,9 +630,9 @@
         name="outer_passes",
     )(far_rows, *far_strips, ground, surface, other)
 
+    floors = lax.all_gather(level, device_axes, axis=0, tiled=True)
     far_rows = lax.ppermute(far, ("rows", "sub"), far_pairs)
     near_rows = lax.ppermute(near, ("rows", "sub"), near_pairs)
-    level = share_levels(level)
 
     def late(*refs):
         late_kernel(height, tiles, *refs)
@@ -715,7 +651,7 @@
         compiler_params=limit,
         cost_estimate=short,
         name="final_passes",
-    )(ground, surface, far_rows, near_rows, level, hops)
+    )(ground, surface, far_rows, near_rows, floors, hops)
 
 
 def solution(mesh):

time: 36 us -> 44.8 us (1.24)
  the two profiles are of different devices: /device:TPU:1 before, /device:TPU:0 now
where the time goes in v1:
time: 44.8 us; the launch traced here: 44.5 us
  blocking collectives  19.3 us (43%)
  Pallas kernels  11.4 us (25%)
  starting transfers between devices  11.1 us (25%)
  waiting for transfers between devices  2.56 us (6%)
    all_gather x1, blocking collectives, per_device(): floors = lax.all_gather(level, device_axes, axis=0, tiled=True)  19.3 us
    ppermute x3, starting transfers between devices, swap_strips(): arrived.append(lax.ppermute(piece, device_axes, pairs) if pairs else piece)  6.27 us
    pallas_call x1, Pallas kernels, per_device(): pl.pallas_call(inner_kernel, out_shape=[work, work, work, pltpu.VMEM((9 *...  5.06 us
    ppermute x2, starting transfers between devices, per_device(): near_rows = lax.ppermute(near, ('rows', 'sub'), near_pairs)  3.51 us
    pallas_call x1, Pallas kernels, per_device(): pl.pallas_call(late, out_shape=jax.ShapeDtypeStruct((height, width), f32)...  2.56 us
    ppermute x3, waiting for transfers between devices, swap_strips(): arrived.append(lax.ppermute(piece, device_axes, pairs) if pairs else piece)  2.55 us
    pallas_call x1, Pallas kernels, per_device(): pl.pallas_call(edge_kernel, out_shape=[sent, sent, far_strip, far_strip,...  1.99 us
    pallas_call x1, Pallas kernels, per_device(): pl.pallas_call(outer, out_shape=[work, work, work, pltpu.VMEM((SUBS, LANE...  1.82 us
  transfers between devices with their start and end apart: 7, of which 2 were waited for; matrix products, arithmetic and copies ran while one was open for 0% of the time, Pallas kernels for 11%

profile of v1, /device:TPU:0, one launch (start us, length us, event | category | flops | bytes accessed | tf_op | source)
XLA Modules:
  0.0 44.5 jit_solution(460554933002629411)
XLA Ops:
  0.0 2.0 %edge_rows.1 = (f32[960,128]{1,0:T(8,128)S(1)}, f32[960,128]{1,0:T(8,128)S(1)}, f32[16,128]{1,0:T(8,128)S(1)}, f32[16,128]{1,0:T(8,128)S(1)}, f32[32,128]{1,0:T(8,128)S(1)}, /*index=5*/f32[32,128]{1,0:T(8,128)S(1)}) custom-call(f32[16,8192]{1,0:T(8,128)} %ground_hbm.3, f32[16,8192]{1,0:T(8,128)} %depth_hbm.3, s32[2,8192]{1,0:T(2,128)} %rows_hbm.3, ...), custom_call_target="tpu_custom_call" | custom-call | flops 1024 | bytes 1024 | tf_op jit(solution)/shard_map/edge_rows/pallas_call | solution.py:563
  2.0 0.5 %collective-permute-start.2 = (f32[960,128]{1,0:T(8,128)S(1)}, f32[960,128]{1,0:T(8,128)S(1)}, u32[]{:S(2)}, u32[]{:S(2)}) collective-permute-start(f32[960,128]{1,0:T(8,128)S(1)} %get-tuple-element.23), channel_id=1, source_target_pairs={{0,1},{1,0},{4,5},{5,4},{8,9},{9,8},{12,13},{13,12},{2,3},{3,2},{6... | collective-permute-start | bytes 1474568 | tf_op jit(solution)/shard_map/ppermute | solution.py:595
  2.5 0.7 %collective-permute-start = (f32[960,128]{1,0:T(8,128)S(1)}, f32[960,128]{1,0:T(8,128)S(1)}, u32[]{:S(2)}, u32[]{:S(2)}) collective-permute-start(f32[960,128]{1,0:T(8,128)S(1)} %get-tuple-element.20), channel_id=1, source_target_pairs={{1,4},{4,1},{5,8},{8,5},{9,12},{12,9},{3,6},{6,3},{7,10},{10,7},{1... | collective-permute-start | bytes 1474568 | tf_op jit(solution)/shard_map/ppermute | solution.py:594
  3.2 5.1 %collective-permute-start.4 = (f32[32,128]{1,0:T(8,128)S(1)}, f32[32,128]{1,0:T(8,128)S(1)}, u32[]{:S(2)}, u32[]{:S(2)}) collective-permute-start(f32[32,128]{1,0:T(8,128)S(1)} %get-tuple-element.24), channel_id=1, source_target_pairs={{0,3},{2,1},{1,2},{3,0},{4,7},{6,5},{5,6},{7,4},{8,11},{10,9},{9,1... | collective-permute-start | bytes 49160 | tf_op jit(solution)/shard_map/ppermute | solution.py:590
  8.3 0.5 %collective-permute-start.3 = (f32[32,128]{1,0:T(8,128)S(1)}, f32[32,128]{1,0:T(8,128)S(1)}, u32[]{:S(2)}, u32[]{:S(2)}) collective-permute-start(f32[32,128]{1,0:T(8,128)S(1)} %get-tuple-element.24), channel_id=1, source_target_pairs={{0,2},{2,0},{1,3},{3,1},{4,6},{6,4},{5,7},{7,5},{8,10},{10,8},{9,1... | collective-permute-start | bytes 49160 | tf_op jit(solution)/shard_map/ppermute | solution.py:590
  8.8 0.6 %collective-permute-start.1 = (f32[16,128]{1,0:T(8,128)S(1)}, f32[16,128]{1,0:T(8,128)S(1)}, u32[]{:S(2)}, u32[]{:S(2)}) collective-permute-start(f32[16,128]{1,0:T(8,128)S(1)} %get-tuple-element.21), channel_id=1, source_target_pairs={{1,6},{3,4},{4,3},{6,1},{5,10},{7,8},{8,7},{10,5},{9,14},{11,12},{... | collective-permute-start | bytes 24584 | tf_op jit(solution)/shard_map/ppermute | solution.py:590
  9.5 0.3 collective-permute-done.4.near_even_ref
  9.7 2.3 %collective-permute-done.3.own_even_ref = f32[32,128]{1,0:T(8,128)S(1)} collective-permute-done((f32[32,128]{1,0:T(8,128)S(1)}, f32[32,128]{1,0:T(8,128)S(1)}, u32[]{:S(2)}, u32[]{:S(2)}) %collective-permute-start.3) | collective-permute-done | bytes 16416 | tf_op jit(solution)/shard_map/ppermute | solution.py:590
  12.0 0.0 collective-permute-done.2.near_ref
  12.0 5.1 %inner_passes.1 = (f32[2304,128]{1,0:T(8,128)S(1)}, f32[2304,128]{1,0:T(8,128)S(1)}, f32[2304,128]{1,0:T(8,128)S(1)}, f32[72,128]{1,0:T(8,128)S(1)}) custom-call(f32[16,8192]{1,0:T(8,128)} %ground_hbm.3, f32[16,8192]{1,0:T(8,128)} %depth_hbm.3, s32[2,8192]{1,0:T(2,128)} %rows_hbm.3, s32[2,16]{1,0:T(2,128)} %sides_hbm.3, s32[8,6]{1,0:T(8,128)} %links_hbm.1, ...), custom_call_target="tpu_custom_call" | custom-call | flops 1024 | bytes 1024 | tf_op jit(solution)/shard_map/inner_passes/pallas_call | solution.py:599
  17.1 0.0 collective-permute-done.1.refs_0_
  17.1 0.0 collective-permute-done.far_ref
  17.1 1.8 %outer_passes.1 = (f32[2304,128]{1,0:T(8,128)S(1)}, f32[2304,128]{1,0:T(8,128)S(1)}, f32[2304,128]{1,0:T(8,128)S(1)}, f32[8,128]{1,0:T(8,128)S(1)}, f32[288,128]{1,0:T(8,128)S(1)}, /*index=5*/f32[288,128]{1,0:T(8,128)S(1)}) custom-call(f32[960,128]{1,0:T(8,128)S(1)} %collective-permute-done.far_ref, ...), custom_call_target="tpu_custom_call", output_to_operand_aliasing={{0}: (3, {}), {1}: (4, {}), {2}: (5, {})} | custom-call | flops 1024 | bytes 1024 | tf_op jit(solution)/shard_map/outer_passes/pallas_call | solution.py:622
  18.9 0.7 %collective-permute-start.5 = (f32[288,128]{1,0:T(8,128)S(1)}, f32[288,128]{1,0:T(8,128)S(1)}, u32[]{:S(2)}, u32[]{:S(2)}) collective-permute-start(f32[288,128]{1,0:T(8,128)S(1)} %get-tuple-element.31), channel_id=1, source_target_pairs={{1,4},{4,1},{5,8},{8,5},{9,12},{12,9},{3,6},{6,3},{7,10},{10,7},{1... | collective-permute-start | bytes 442376 | tf_op jit(solution)/shard_map/ppermute | solution.py:634
  19.6 3.0 %collective-permute-start.6 = (f32[288,128]{1,0:T(8,128)S(1)}, f32[288,128]{1,0:T(8,128)S(1)}, u32[]{:S(2)}, u32[]{:S(2)}) collective-permute-start(f32[288,128]{1,0:T(8,128)S(1)} %get-tuple-element.32), channel_id=1, source_target_pairs={{0,1},{1,0},{4,5},{5,4},{8,9},{9,8},{12,13},{13,12},{2,3},{3,2},{6... | collective-permute-start | bytes 442376 | tf_op jit(solution)/shard_map/ppermute | solution.py:635
  22.6 19.3 %all_gather.3.refs_4_ = f32[128,128]{1,0:T(8,128)S(1)} all-gather(f32[8,128]{1,0:T(8,128)S(1)} %get-tuple-element.33), channel_id=1, replica_groups=mesh['groups'=2,'rows'=4,'cols'=2,'sub'=2] {'rows','cols','sub'}, dimensions={0}, use_global_device_ids=true | all-gather | bytes 69632 | tf_op jit(solution)/shard_map/all_gather | solution.py:633
  41.9 0.0 collective-permute-done.5.refs_2_
  42.0 0.0 collective-permute-done.6.refs_3_
  42.0 2.6 %final_passes.1 = f32[16,8192]{1,0:T(8,128)} custom-call(f32[2304,128]{1,0:T(8,128)S(1)} %get-tuple-element.29.refs_0_, f32[2304,128]{1,0:T(8,128)S(1)} %get-tuple-element.30.refs_1_, f32[288,128]{1,0:T(8,128)S(1)} %collective-permute-done.5.refs_2_, f32[288,128]{1,0:T(8,128)S(1)} %collective-permute-done.6.refs_3_, f32[128,128]{1,0:T(8,128)S(1)} %all_gather.3.refs_4_, ...), custom_call_target="tpu_custom_call" | custom-call | flops 1024 | bytes 1024 | tf_op jit(solution)/shard_map/final_passes/pallas_call | solution.py:640
Async XLA Ops:
  2.0 10.0 %collective-permute-start.2 = (f32[960,128]{1,0:T(8,128)S(1)}, f32[960,128]{1,0:T(8,128)S(1)}, u32[]{:S(2)}, u32[]{:S(2)}) collective-permute-start(f32[960,128]{1,0:T(8,128)S(1)} %get-tuple-element.23), channel_id=1, source_target_pairs={{0,1},{1,0},{4,5},{5,4},{8,9},{9,8},{12,13},{13,12},{2,3},{3,2},{6... | collective-permute-start | bytes 1474568 | tf_op jit(solution)/shard_map/ppermute | solution.py:595
  2.5 14.6 %collective-permute-start = (f32[960,128]{1,0:T(8,128)S(1)}, f32[960,128]{1,0:T(8,128)S(1)}, u32[]{:S(2)}, u32[]{:S(2)}) collective-permute-start(f32[960,128]{1,0:T(8,128)S(1)} %get-tuple-element.20), channel_id=1, source_target_pairs={{1,4},{4,1},{5,8},{8,5},{9,12},{12,9},{3,6},{6,3},{7,10},{10,7},{1... | collective-permute-start | bytes 1474568 | tf_op jit(solution)/shard_map/ppermute | solution.py:594
  3.2 6.5 %collective-permute-start.4 = (f32[32,128]{1,0:T(8,128)S(1)}, f32[32,128]{1,0:T(8,128)S(1)}, u32[]{:S(2)}, u32[]{:S(2)}) collective-permute-start(f32[32,128]{1,0:T(8,128)S(1)} %get-tuple-element.24), channel_id=1, source_target_pairs={{0,3},{2,1},{1,2},{3,0},{4,7},{6,5},{5,6},{7,4},{8,11},{10,9},{9,1... | collective-permute-start | bytes 49160 | tf_op jit(solution)/shard_map/ppermute | solution.py:590
  8.3 3.7 %collective-permute-start.3 = (f32[32,128]{1,0:T(8,128)S(1)}, f32[32,128]{1,0:T(8,128)S(1)}, u32[]{:S(2)}, u32[]{:S(2)}) collective-permute-start(f32[32,128]{1,0:T(8,128)S(1)} %get-tuple-element.24), channel_id=1, source_target_pairs={{0,2},{2,0},{1,3},{3,1},{4,6},{6,4},{5,7},{7,5},{8,10},{10,8},{9,1... | collective-permute-start | bytes 49160 | tf_op jit(solution)/shard_map/ppermute | solution.py:590
  8.8 8.3 %collective-permute-start.1 = (f32[16,128]{1,0:T(8,128)S(1)}, f32[16,128]{1,0:T(8,128)S(1)}, u32[]{:S(2)}, u32[]{:S(2)}) collective-permute-start(f32[16,128]{1,0:T(8,128)S(1)} %get-tuple-element.21), channel_id=1, source_target_pairs={{1,6},{3,4},{4,3},{6,1},{5,10},{7,8},{8,7},{10,5},{9,14},{11,12},{... | collective-permute-start | bytes 24584 | tf_op jit(solution)/shard_map/ppermute | solution.py:590
  18.9 23.0 %collective-permute-start.5 = (f32[288,128]{1,0:T(8,128)S(1)}, f32[288,128]{1,0:T(8,128)S(1)}, u32[]{:S(2)}, u32[]{:S(2)}) collective-permute-start(f32[288,128]{1,0:T(8,128)S(1)} %get-tuple-element.31), channel_id=1, source_target_pairs={{1,4},{4,1},{5,8},{8,5},{9,12},{12,9},{3,6},{6,3},{7,10},{10,7},{1... | collective-permute-start | bytes 442376 | tf_op jit(solution)/shard_map/ppermute | solution.py:634
  19.6 22.3 %collective-permute-start.6 = (f32[288,128]{1,0:T(8,128)S(1)}, f32[288,128]{1,0:T(8,128)S(1)}, u32[]{:S(2)}, u32[]{:S(2)}) collective-permute-start(f32[288,128]{1,0:T(8,128)S(1)} %get-tuple-element.32), channel_id=1, source_target_pairs={{0,1},{1,0},{4,5},{5,4},{8,9},{9,8},{12,13},{13,12},{2,3},{3,2},{6... | collective-permute-start | bytes 442376 | tf_op jit(solution)/shard_map/ppermute | solution.py:635

commit v2 on v1

--- a/solution.py
+++ b/solution.py
@@ -23,6 +23,11 @@
     for low in range(first, count - 1, 2):
         pairs += [(low, low + 1), (low + 1, low)]
     return pairs
+
+
+def closed(pairs, count):
+    used = {source for source, _ in pairs}
+    return pairs + [(place, place) for place in range(count) if place not in used]
 
 
 def cross(row_pairs, col_pairs, cols, subs):
@@ -448,7 +453,9 @@
         ),
     )
     lowest = jnp.min(jnp.min(lowest, axis=0, keepdims=True), axis=1, keepdims=True)
-    level_ref[...] = jnp.broadcast_to(lowest, level_ref.shape)
+    tile_id = lax.axis_index("rows") * lax.axis_size("cols") + lax.axis_index("cols")
+    number = lax.broadcasted_iota(jnp.int32, level_ref.shape, 0)
+    level_ref[...] = jnp.where(number == tile_id, lowest, unreached)
 
 
 def least(values):
@@ -462,7 +469,7 @@
 
 
 def late_kernel(
-    height, tiles, ground_ref, surface_ref, far_ref, near_ref, floors_ref, hops_ref, out_hbm,
+    height, tiles, ground_ref, surface_ref, far_ref, near_ref, level_ref, hops_ref, out_hbm,
     one_ref, two_ref, out_ref, sems,
 ):
     ring = tiles + 1
@@ -470,9 +477,8 @@
     sub, lane = position()
     place, _ = chain_place()
     top = place % 2 == 0
-    bands = lax.axis_size("sub")
-    count = floors_ref.shape[0] // (bands * SUBS)
-    level = least(floors_ref[pl.ds(band * SUBS, count, stride=bands * SUBS), :] for band in range(bands))
+    level = level_ref[...]
+    count = level.shape[0]
     raised = [level]
     for hop in range(ROUNDS):
         raised.append(raised[-1] + hop_rise)
@@ -539,6 +545,51 @@
 
 def in_hbm(count):
     return [pl.BlockSpec(memory_space=pltpu.HBM)] * count
+
+
+def exchange_stages(rows, cols, subs):
+    bits = []
+    for axis, count in enumerate((rows, cols, subs)):
+        bit = 1
+        while bit < count:
+            bits.append((axis, bit))
+            bit *= 2
+    bits.reverse()
+    stages = []
+    for first in range(0, len(bits), 2):
+        group = bits[first : first + 2]
+        shifts = []
+        for chosen in range(1, 2 ** len(group)):
+            shift = [0, 0, 0]
+            for number, (axis, bit) in enumerate(group):
+                if chosen >> number & 1:
+                    shift[axis] ^= bit
+            shifts.append(shift)
+        stages.append(shifts)
+    return stages
+
+
+def share_levels(level, rows_arriving):
+    rows, cols, subs = [lax.axis_size(axis) for axis in ("rows", "cols", "sub")]
+    if any(count & (count - 1) for count in (rows, cols, subs)):
+        return lax.pmin(level, ("rows", "cols", "sub")), rows_arriving
+    for number, shifts in enumerate(exchange_stages(rows, cols, subs)):
+        arrived = [level]
+        for down, across, core in shifts:
+            pairs = [
+                (
+                    (row * cols + col) * subs + sub,
+                    ((row ^ down) * cols + (col ^ across)) * subs + (sub ^ core),
+                )
+                for row in range(rows)
+                for col in range(cols)
+                for sub in range(subs)
+            ]
+            arrived.append(lax.ppermute(level, ("rows", "cols", "sub"), pairs))
+        level = least(arrived)
+        if number == 0:
+            level, *rows_arriving = lax.optimization_barrier((level, *rows_arriving))
+    return level, rows_arriving
 
 
 def per_device(elevation, fill_depth, edge_rows, edge_sides, adjacency):
@@ -579,7 +630,7 @@
         name="edge_rows",
     )(*arguments[:4])
 
-    near_pairs, far_pairs = matching(places, 0), matching(places, 1)
+    near_pairs, far_pairs = [closed(matching(places, first), places) for first in range(2)]
     stay = [(place, place) for place in range(places)]
     device_axes = ("rows", "cols", "sub")
 
@@ -621,7 +672,7 @@
     again = pltpu.VMEM((FINAL * size, LANES), f32)
     ground, surface, other, level, far, near = pl.pallas_call(
         outer,
-        out_shape=[work, work, work, pltpu.VMEM((SUBS, LANES), f32), again, again],
+        out_shape=[work, work, work, pltpu.VMEM((tile_count, LANES), f32), again, again],
         in_specs=in_vmem(6),
         out_specs=in_vmem(6),
         input_output_aliases={3: 0, 4: 1, 5: 2},
@@ -630,9 +681,9 @@
         name="outer_passes",
     )(far_rows, *far_strips, ground, surface, other)
 
-    floors = lax.all_gather(level, device_axes, axis=0, tiled=True)
     far_rows = lax.ppermute(far, ("rows", "sub"), far_pairs)
     near_rows = lax.ppermute(near, ("rows", "sub"), near_pairs)
+    level, (far_rows, near_rows) = share_levels(level, (far_rows, near_rows))
 
     def late(*refs):
         late_kernel(height, tiles, *refs)
@@ -651,7 +702,7 @@
         compiler_params=limit,
         cost_estimate=short,
         name="final_passes",
-    )(ground, surface, far_rows, near_rows, floors, hops)
+    )(ground, surface, far_rows, near_rows, level, hops)
 
 
 def solution(mesh):

time: 44.8 us -> 37.8 us (0.84)
  blocking collectives: 19.3 us -> 0 us
  starting transfers between devices: 11.1 us -> 18.8 us
  waiting for transfers between devices: 2.56 us -> 7.2 us
    all_gather x1 -> x0, blocking collectives: 19.3 us -> none  [per_device(): floors = lax.all_gather(level, device_axes, axis=0, tiled=True)]
    ppermute x0 -> x6, starting transfers between devices: none -> 6.84 us  [share_levels(): arrived.append(lax.ppermute(level, ('rows', 'cols', 'sub'), pairs))]
    ppermute x0 -> x6, waiting for transfers between devices: none -> 4.51 us  [share_levels(): arrived.append(lax.ppermute(level, ('rows', 'cols', 'sub'), pairs))]
    ppermute x2, waiting for transfers between devices: 0.01 us -> 0.97 us  [per_device(): near_rows = lax.ppermute(near, ('rows', 'sub'), near_pairs)]
    ppermute x3, starting transfers between devices: 6.27 us -> 7.11 us  [swap_strips(): arrived.append(lax.ppermute(piece, device_axes, pairs) if pairs else piece)]
    ppermute x3, waiting for transfers between devices: 2.55 us -> 1.71 us  [swap_strips(): arrived.append(lax.ppermute(piece, device_axes, pairs) if pairs else piece)]
  transfers between devices with their start and end apart: 7 -> 13, of which waited for: 2 -> 5; matrix products, arithmetic and copies ran while one was open for 0% -> 0% of each run, Pallas kernels for 11% -> 13%
where the time goes in v2:
time: 37.8 us; the launch traced here: 37.5 us
  starting transfers between devices  18.8 us (50%)
  Pallas kernels  11.4 us (30%)
  waiting for transfers between devices  7.2 us (19%)
    ppermute x3, starting transfers between devices, swap_strips(): arrived.append(lax.ppermute(piece, device_axes, pairs) if pairs else piece)  7.11 us
    ppermute x6, starting transfers between devices, share_levels(): arrived.append(lax.ppermute(level, ('rows', 'cols', 'sub'), pairs))  6.84 us
    pallas_call x1, Pallas kernels, per_device(): pl.pallas_call(inner_kernel, out_shape=[work, work, work, pltpu.VMEM((9 *...  5.06 us
    ppermute x6, waiting for transfers between devices, share_levels(): arrived.append(lax.ppermute(level, ('rows', 'cols', 'sub'), pairs))  4.51 us
    ppermute x2, starting transfers between devices, per_device(): near_rows = lax.ppermute(near, ('rows', 'sub'), near_pairs)  3.51 us
    pallas_call x1, Pallas kernels, per_device(): pl.pallas_call(late, out_shape=jax.ShapeDtypeStruct((height, width), f32)...  2.56 us
    pallas_call x1, Pallas kernels, per_device(): pl.pallas_call(edge_kernel, out_shape=[sent, sent, far_strip, far_strip,...  1.99 us
    pallas_call x1, Pallas kernels, per_device(): pl.pallas_call(outer, out_shape=[work, work, work, pltpu.VMEM((tile_count...  1.82 us
  transfers between devices with their start and end apart: 13, of which 5 were waited for; matrix products, arithmetic and copies ran while one was open for 0% of the time, Pallas kernels for 13%

profile of v2, /device:TPU:0, one launch (start us, length us, event | category | flops | bytes accessed | tf_op | source)
XLA Modules:
  0.0 37.5 jit_solution(1467998080848352136)
XLA Ops:
  0.0 2.0 %edge_rows.1 = (f32[960,128]{1,0:T(8,128)S(1)}, f32[960,128]{1,0:T(8,128)S(1)}, f32[16,128]{1,0:T(8,128)S(1)}, f32[16,128]{1,0:T(8,128)S(1)}, f32[32,128]{1,0:T(8,128)S(1)}, /*index=5*/f32[32,128]{1,0:T(8,128)S(1)}) custom-call(f32[16,8192]{1,0:T(8,128)} %ground_hbm.3, f32[16,8192]{1,0:T(8,128)} %depth_hbm.3, s32[2,8192]{1,0:T(2,128)} %rows_hbm.3, ...), custom_call_target="tpu_custom_call" | custom-call | flops 1024 | bytes 1024 | tf_op jit(solution)/shard_map/edge_rows/pallas_call | solution.py:614
  2.0 0.5 %collective-permute-start.2 = (f32[960,128]{1,0:T(8,128)S(1)}, f32[960,128]{1,0:T(8,128)S(1)}, u32[]{:S(2)}, u32[]{:S(2)}) collective-permute-start(f32[960,128]{1,0:T(8,128)S(1)} %get-tuple-element.26), channel_id=1, source_target_pairs={{0,1},{1,0},{4,5},{5,4},{8,9},{9,8},{12,13},{13,12},{2,3},{3,2},{6... | collective-permute-start | bytes 1474568 | tf_op jit(solution)/shard_map/ppermute | solution.py:646
  2.5 0.7 %collective-permute-start = (f32[960,128]{1,0:T(8,128)S(1)}, f32[960,128]{1,0:T(8,128)S(1)}, u32[]{:S(2)}, u32[]{:S(2)}) collective-permute-start(f32[960,128]{1,0:T(8,128)S(1)} %get-tuple-element.23), channel_id=1, source_target_pairs={{1,4},{4,1},{5,8},{8,5},{9,12},{12,9},{0,0},{13,13},{3,6},{6,3},{7... | collective-permute-start | bytes 1474568 | tf_op jit(solution)/shard_map/ppermute | solution.py:645
  3.2 5.1 %collective-permute-start.4 = (f32[32,128]{1,0:T(8,128)S(1)}, f32[32,128]{1,0:T(8,128)S(1)}, u32[]{:S(2)}, u32[]{:S(2)}) collective-permute-start(f32[32,128]{1,0:T(8,128)S(1)} %get-tuple-element.27), channel_id=1, source_target_pairs={{0,3},{2,1},{1,2},{3,0},{4,7},{6,5},{5,6},{7,4},{8,11},{10,9},{9,1... | collective-permute-start | bytes 49160 | tf_op jit(solution)/shard_map/ppermute | solution.py:641
  8.3 0.5 %collective-permute-start.3 = (f32[32,128]{1,0:T(8,128)S(1)}, f32[32,128]{1,0:T(8,128)S(1)}, u32[]{:S(2)}, u32[]{:S(2)}) collective-permute-start(f32[32,128]{1,0:T(8,128)S(1)} %get-tuple-element.27), channel_id=1, source_target_pairs={{0,2},{2,0},{1,3},{3,1},{4,6},{6,4},{5,7},{7,5},{8,10},{10,8},{9,1... | collective-permute-start | bytes 49160 | tf_op jit(solution)/shard_map/ppermute | solution.py:641
  8.8 1.5 %collective-permute-start.1 = (f32[16,128]{1,0:T(8,128)S(1)}, f32[16,128]{1,0:T(8,128)S(1)}, u32[]{:S(2)}, u32[]{:S(2)}) collective-permute-start(f32[16,128]{1,0:T(8,128)S(1)} %get-tuple-element.24), channel_id=1, source_target_pairs={{1,6},{3,4},{4,3},{6,1},{5,10},{7,8},{8,7},{10,5},{9,14},{11,12},{... | collective-permute-start | bytes 24584 | tf_op jit(solution)/shard_map/ppermute | solution.py:641
  10.3 0.0 collective-permute-done.4.near_even_ref
  10.3 1.7 %collective-permute-done.3.own_even_ref = f32[32,128]{1,0:T(8,128)S(1)} collective-permute-done((f32[32,128]{1,0:T(8,128)S(1)}, f32[32,128]{1,0:T(8,128)S(1)}, u32[]{:S(2)}, u32[]{:S(2)}) %collective-permute-start.3) | collective-permute-done | bytes 16416 | tf_op jit(solution)/shard_map/ppermute | solution.py:641
  12.0 0.0 collective-permute-done.2.near_ref
  12.0 5.1 %inner_passes.1 = (f32[2304,128]{1,0:T(8,128)S(1)}, f32[2304,128]{1,0:T(8,128)S(1)}, f32[2304,128]{1,0:T(8,128)S(1)}, f32[72,128]{1,0:T(8,128)S(1)}) custom-call(f32[16,8192]{1,0:T(8,128)} %ground_hbm.3, f32[16,8192]{1,0:T(8,128)} %depth_hbm.3, s32[2,8192]{1,0:T(2,128)} %rows_hbm.3, s32[2,16]{1,0:T(2,128)} %sides_hbm.3, s32[8,6]{1,0:T(8,128)} %links_hbm.1, ...), custom_call_target="tpu_custom_call" | custom-call | flops 1024 | bytes 1024 | tf_op jit(solution)/shard_map/inner_passes/pallas_call | solution.py:650
  17.1 0.0 collective-permute-done.1.refs_0_
  17.1 0.0 collective-permute-done.far_ref
  17.1 1.8 %outer_passes.1 = (f32[2304,128]{1,0:T(8,128)S(1)}, f32[2304,128]{1,0:T(8,128)S(1)}, f32[2304,128]{1,0:T(8,128)S(1)}, f32[8,128]{1,0:T(8,128)S(1)}, f32[288,128]{1,0:T(8,128)S(1)}, /*index=5*/f32[288,128]{1,0:T(8,128)S(1)}) custom-call(f32[960,128]{1,0:T(8,128)S(1)} %collective-permute-done.far_ref, ...), custom_call_target="tpu_custom_call", output_to_operand_aliasing={{0}: (3, {}), {1}: (4, {}), {2}: (5, {})} | custom-call | flops 1024 | bytes 1024 | tf_op jit(solution)/shard_map/outer_passes/pallas_call | solution.py:673
  18.9 0.0 collective-permute-start.7
  19.0 1.0 %collective-permute-start.6 = (f32[8,128]{1,0:T(8,128)S(1)}, f32[8,128]{1,0:T(8,128)S(1)}, u32[]{:S(2)}, u32[]{:S(2)}) collective-permute-start(f32[8,128]{1,0:T(8,128)S(1)} %get-tuple-element.34), channel_id=1, source_target_pairs={{0,2},{1,3},{2,0},{3,1},{4,6},{5,7},{6,4},{7,5},{8,10},{9,11},{10,... | collective-permute-start | bytes 12296 | tf_op jit(solution)/shard_map/ppermute | solution.py:588
  20.0 0.8 %collective-permute-start.5 = (f32[8,128]{1,0:T(8,128)S(1)}, f32[8,128]{1,0:T(8,128)S(1)}, u32[]{:S(2)}, u32[]{:S(2)}) collective-permute-start(f32[8,128]{1,0:T(8,128)S(1)} %get-tuple-element.34), channel_id=1, source_target_pairs={{0,1},{1,0},{2,3},{3,2},{4,5},{5,4},{6,7},{7,6},{8,9},{9,8},{10,11... | collective-permute-start | bytes 12296 | tf_op jit(solution)/shard_map/ppermute | solution.py:588
  20.8 0.7 %collective-permute-start.8 = (f32[288,128]{1,0:T(8,128)S(1)}, f32[288,128]{1,0:T(8,128)S(1)}, u32[]{:S(2)}, u32[]{:S(2)}) collective-permute-start(f32[288,128]{1,0:T(8,128)S(1)} %get-tuple-element.35), channel_id=1, source_target_pairs={{1,4},{4,1},{5,8},{8,5},{9,12},{12,9},{0,0},{13,13},{3,6},{6,3},{7... | collective-permute-start | bytes 442376 | tf_op jit(solution)/shard_map/ppermute | solution.py:684
  21.5 3.0 %collective-permute-start.9 = (f32[288,128]{1,0:T(8,128)S(1)}, f32[288,128]{1,0:T(8,128)S(1)}, u32[]{:S(2)}, u32[]{:S(2)}) collective-permute-start(f32[288,128]{1,0:T(8,128)S(1)} %get-tuple-element.36), channel_id=1, source_target_pairs={{0,1},{1,0},{4,5},{5,4},{8,9},{9,8},{12,13},{13,12},{2,3},{3,2},{6... | collective-permute-start | bytes 442376 | tf_op jit(solution)/shard_map/ppermute | solution.py:685
  24.5 0.0 collective-permute-done.7
  24.5 0.0 collective-permute-done.6
  24.5 0.0 collective-permute-done.5
  24.5 0.0 collective-permute-done.8.refs_2_
  24.5 1.0 %collective-permute-done.9.refs_3_ = f32[288,128]{1,0:T(8,128)S(1)} collective-permute-done((f32[288,128]{1,0:T(8,128)S(1)}, f32[288,128]{1,0:T(8,128)S(1)}, u32[]{:S(2)}, u32[]{:S(2)}) %collective-permute-start.9) | collective-permute-done | bytes 147488 | tf_op jit(solution)/shard_map/ppermute | solution.py:685
  25.5 3.7 %collective-permute-start.12 = (f32[8,128]{1,0:T(8,128)S(1)}, f32[8,128]{1,0:T(8,128)S(1)}, u32[]{:S(2)}, u32[]{:S(2)}) collective-permute-start(f32[8,128]{1,0:T(8,128)S(1)} %minimum_minimum_fusion.1), channel_id=1, source_target_pairs={{0,12},{1,13},{2,14},{3,15},{4,8},{5,9},{6,10},{7,11},{8,4},{9,5},... | collective-permute-start | bytes 12296 | tf_op jit(solution)/shard_map/ppermute | solution.py:588
  29.2 1.2 %collective-permute-start.11 = (f32[8,128]{1,0:T(8,128)S(1)}, f32[8,128]{1,0:T(8,128)S(1)}, u32[]{:S(2)}, u32[]{:S(2)}) collective-permute-start(f32[8,128]{1,0:T(8,128)S(1)} %minimum_minimum_fusion.1), channel_id=1, source_target_pairs={{0,4},{1,5},{2,6},{3,7},{4,0},{5,1},{6,2},{7,3},{8,12},{9,13},{10,... | collective-permute-start | bytes 12296 | tf_op jit(solution)/shard_map/ppermute | solution.py:588
  30.5 0.0 collective-permute-start.10
  30.5 0.5 %collective-permute-done.12 = f32[8,128]{1,0:T(8,128)S(1)} collective-permute-done((f32[8,128]{1,0:T(8,128)S(1)}, f32[8,128]{1,0:T(8,128)S(1)}, u32[]{:S(2)}, u32[]{:S(2)}) %collective-permute-start.12) | collective-permute-done | bytes 4128 | tf_op jit(solution)/shard_map/ppermute | solution.py:588
  30.9 1.9 %collective-permute-done.11 = f32[8,128]{1,0:T(8,128)S(1)} collective-permute-done((f32[8,128]{1,0:T(8,128)S(1)}, f32[8,128]{1,0:T(8,128)S(1)}, u32[]{:S(2)}, u32[]{:S(2)}) %collective-permute-start.11) | collective-permute-done | bytes 4128 | tf_op jit(solution)/shard_map/ppermute | solution.py:588
  32.8 2.1 %collective-permute-done.10 = f32[8,128]{1,0:T(8,128)S(1)} collective-permute-done((f32[8,128]{1,0:T(8,128)S(1)}, f32[8,128]{1,0:T(8,128)S(1)}, u32[]{:S(2)}, u32[]{:S(2)}) %collective-permute-start.10) | collective-permute-done | bytes 4128 | tf_op jit(solution)/shard_map/ppermute | solution.py:588
  35.0 2.6 %final_passes.1 = f32[16,8192]{1,0:T(8,128)} custom-call(f32[2304,128]{1,0:T(8,128)S(1)} %get-tuple-element.32.refs_0_, f32[2304,128]{1,0:T(8,128)S(1)} %get-tuple-element.33.refs_1_, f32[288,128]{1,0:T(8,128)S(1)} %collective-permute-done.8.refs_2_, f32[288,128]{1,0:T(8,128)S(1)} %collective-permute-done.9.refs_3_, ...), custom_call_target="tpu_custom_call" | custom-call | flops 1024 | bytes 1024 | tf_op jit(solution)/shard_map/final_passes/pallas_call | solution.py:691
  (2 shorter events, 0.0 us)
Async XLA Ops:
  2.0 10.0 %collective-permute-start.2 = (f32[960,128]{1,0:T(8,128)S(1)}, f32[960,128]{1,0:T(8,128)S(1)}, u32[]{:S(2)}, u32[]{:S(2)}) collective-permute-start(f32[960,128]{1,0:T(8,128)S(1)} %get-tuple-element.26), channel_id=1, source_target_pairs={{0,1},{1,0},{4,5},{5,4},{8,9},{9,8},{12,13},{13,12},{2,3},{3,2},{6... | collective-permute-start | bytes 1474568 | tf_op jit(solution)/shard_map/ppermute | solution.py:646
  2.5 14.6 %collective-permute-start = (f32[960,128]{1,0:T(8,128)S(1)}, f32[960,128]{1,0:T(8,128)S(1)}, u32[]{:S(2)}, u32[]{:S(2)}) collective-permute-start(f32[960,128]{1,0:T(8,128)S(1)} %get-tuple-element.23), channel_id=1, source_target_pairs={{1,4},{4,1},{5,8},{8,5},{9,12},{12,9},{0,0},{13,13},{3,6},{6,3},{7... | collective-permute-start | bytes 1474568 | tf_op jit(solution)/shard_map/ppermute | solution.py:645
  3.2 7.1 %collective-permute-start.4 = (f32[32,128]{1,0:T(8,128)S(1)}, f32[32,128]{1,0:T(8,128)S(1)}, u32[]{:S(2)}, u32[]{:S(2)}) collective-permute-start(f32[32,128]{1,0:T(8,128)S(1)} %get-tuple-element.27), channel_id=1, source_target_pairs={{0,3},{2,1},{1,2},{3,0},{4,7},{6,5},{5,6},{7,4},{8,11},{10,9},{9,1... | collective-permute-start | bytes 49160 | tf_op jit(solution)/shard_map/ppermute | solution.py:641
  8.3 3.7 %collective-permute-start.3 = (f32[32,128]{1,0:T(8,128)S(1)}, f32[32,128]{1,0:T(8,128)S(1)}, u32[]{:S(2)}, u32[]{:S(2)}) collective-permute-start(f32[32,128]{1,0:T(8,128)S(1)} %get-tuple-element.27), channel_id=1, source_target_pairs={{0,2},{2,0},{1,3},{3,1},{4,6},{6,4},{5,7},{7,5},{8,10},{10,8},{9,1... | collective-permute-start | bytes 49160 | tf_op jit(solution)/shard_map/ppermute | solution.py:641
  8.8 8.3 %collective-permute-start.1 = (f32[16,128]{1,0:T(8,128)S(1)}, f32[16,128]{1,0:T(8,128)S(1)}, u32[]{:S(2)}, u32[]{:S(2)}) collective-permute-start(f32[16,128]{1,0:T(8,128)S(1)} %get-tuple-element.24), channel_id=1, source_target_pairs={{1,6},{3,4},{4,3},{6,1},{5,10},{7,8},{8,7},{10,5},{9,14},{11,12},{... | collective-permute-start | bytes 24584 | tf_op jit(solution)/shard_map/ppermute | solution.py:641
  18.9 5.6 %collective-permute-start.7 = (f32[8,128]{1,0:T(8,128)S(1)}, f32[8,128]{1,0:T(8,128)S(1)}, u32[]{:S(2)}, u32[]{:S(2)}) collective-permute-start(f32[8,128]{1,0:T(8,128)S(1)} %get-tuple-element.34), channel_id=1, source_target_pairs={{0,3},{1,2},{2,1},{3,0},{4,7},{5,6},{6,5},{7,4},{8,11},{9,10},{10,... | collective-permute-start | bytes 12296 | tf_op jit(solution)/shard_map/ppermute | solution.py:588
  19.0 5.5 %collective-permute-start.6 = (f32[8,128]{1,0:T(8,128)S(1)}, f32[8,128]{1,0:T(8,128)S(1)}, u32[]{:S(2)}, u32[]{:S(2)}) collective-permute-start(f32[8,128]{1,0:T(8,128)S(1)} %get-tuple-element.34), channel_id=1, source_target_pairs={{0,2},{1,3},{2,0},{3,1},{4,6},{5,7},{6,4},{7,5},{8,10},{9,11},{10,... | collective-permute-start | bytes 12296 | tf_op jit(solution)/shard_map/ppermute | solution.py:588
  20.0 4.5 %collective-permute-start.5 = (f32[8,128]{1,0:T(8,128)S(1)}, f32[8,128]{1,0:T(8,128)S(1)}, u32[]{:S(2)}, u32[]{:S(2)}) collective-permute-start(f32[8,128]{1,0:T(8,128)S(1)} %get-tuple-element.34), channel_id=1, source_target_pairs={{0,1},{1,0},{2,3},{3,2},{4,5},{5,4},{6,7},{7,6},{8,9},{9,8},{10,11... | collective-permute-start | bytes 12296 | tf_op jit(solution)/shard_map/ppermute | solution.py:588
  20.8 3.7 %collective-permute-start.8 = (f32[288,128]{1,0:T(8,128)S(1)}, f32[288,128]{1,0:T(8,128)S(1)}, u32[]{:S(2)}, u32[]{:S(2)}) collective-permute-start(f32[288,128]{1,0:T(8,128)S(1)} %get-tuple-element.35), channel_id=1, source_target_pairs={{1,4},{4,1},{5,8},{8,5},{9,12},{12,9},{0,0},{13,13},{3,6},{6,3},{7... | collective-permute-start | bytes 442376 | tf_op jit(solution)/shard_map/ppermute | solution.py:684
  21.5 4.0 %collective-permute-start.9 = (f32[288,128]{1,0:T(8,128)S(1)}, f32[288,128]{1,0:T(8,128)S(1)}, u32[]{:S(2)}, u32[]{:S(2)}) collective-permute-start(f32[288,128]{1,0:T(8,128)S(1)} %get-tuple-element.36), channel_id=1, source_target_pairs={{0,1},{1,0},{4,5},{5,4},{8,9},{9,8},{12,13},{13,12},{2,3},{3,2},{6... | collective-permute-start | bytes 442376 | tf_op jit(solution)/shard_map/ppermute | solution.py:685
  25.5 5.4 %collective-permute-start.12 = (f32[8,128]{1,0:T(8,128)S(1)}, f32[8,128]{1,0:T(8,128)S(1)}, u32[]{:S(2)}, u32[]{:S(2)}) collective-permute-start(f32[8,128]{1,0:T(8,128)S(1)} %minimum_minimum_fusion.1), channel_id=1, source_target_pairs={{0,12},{1,13},{2,14},{3,15},{4,8},{5,9},{6,10},{7,11},{8,4},{9,5},... | collective-permute-start | bytes 12296 | tf_op jit(solution)/shard_map/ppermute | solution.py:588
  29.2 3.6 %collective-permute-start.11 = (f32[8,128]{1,0:T(8,128)S(1)}, f32[8,128]{1,0:T(8,128)S(1)}, u32[]{:S(2)}, u32[]{:S(2)}) collective-permute-start(f32[8,128]{1,0:T(8,128)S(1)} %minimum_minimum_fusion.1), channel_id=1, source_target_pairs={{0,4},{1,5},{2,6},{3,7},{4,0},{5,1},{6,2},{7,3},{8,12},{9,13},{10,... | collective-permute-start | bytes 12296 | tf_op jit(solution)/shard_map/ppermute | solution.py:588
  30.5 4.5 %collective-permute-start.10 = (f32[8,128]{1,0:T(8,128)S(1)}, f32[8,128]{1,0:T(8,128)S(1)}, u32[]{:S(2)}, u32[]{:S(2)}) collective-permute-start(f32[8,128]{1,0:T(8,128)S(1)} %minimum_minimum_fusion.1), channel_id=1, source_target_pairs={{0,8},{1,9},{2,10},{3,11},{4,12},{5,13},{6,14},{7,15},{8,0},{9,1},... | collective-permute-start | bytes 12296 | tf_op jit(solution)/shard_map/ppermute | solution.py:588
